TPU v7x, 32 devices: a whole 2x2x4 slice. The times are simulated.
32 devices in a mesh: variant: 4 (over y, x), sub: 8 (over z, core).
Axes of the slice: x: 2, y: 2, z: 4, core: 2. Of those that a mesh axis runs over, the one named last changes fastest.
Arguments:
- displacement: float32 [4, 6, 1024], P('variant', None, 'sub'), may hold values from -6 to 6
- neighbours: int32 [2, 1024], P(None, 'sub'), may hold values from 0 to 129, as said below
- micro_state: bfloat16 [4, 24576, 512], P('variant', 'sub'), may hold values from -6 to 6
- strain_loads: float32 [4, 6, 512], P('variant'), may hold values from -3 to 3
- stiffness: bfloat16 [4, 512, 512], P('variant'), may hold values from -0.25 to 0.25
- expand_weight: bfloat16 [4, 512, 2048], P('variant'), may hold values from -0.25 to 0.25
- contract_weight: bfloat16 [4, 2048, 512], P('variant'), may hold values from -0.125 to 0.125
- batch_route: int32 [4, 2, 192], P('variant', None, 'sub'), may hold values from -1 to 7, as said below
- yield_flags: int32 [4, 24576], P('variant', 'sub'), may hold values 0 or 1
- readout: bfloat16 [4, 512], P('variant'), may hold values from -0.75 to 0.75
- external_force: float32 [4, 1024], P('variant', 'sub'), may hold values from -6 to 6
- coarse_inverse: bfloat16 [4, 1024, 1024], P('variant', 'sub'), may hold values from -0.1875 to 0.1875
Outputs:
- states_next: bfloat16 [4, 24576, 512], P('variant', 'sub')
- coarse_correction: float32 [4, 1024], P('variant', 'sub')
Inputs may be any that keep to these rules, and one draw needn't show every extreme that they name: `neighbours`: entry 0 is position i or i + 1 of macro point i within its device (i counted from 0 in the device), entry 1 is i + 1 or i + 2, and entry 1 exceeds entry 0; the first and last point of each device use i and i + 2. `batch_route`: entry 0 of a batch held by device s on sub is -1 or (s + d) % 8 for some d from 1 to 4, each d used by at most one batch of s; entry 1 is -1 where entry 0 is, else its slot there, 0 to 1. Batches sent to one device have different slots; every device receives at most 2 batches, and in every draw some device receives 2.
All inputs are finite; a program needn't handle non-finite values. No bound on the sum of `yield_flags` on one device may be relied on, other than what follows from the above.
Results may differ from a plain program's by a relative error of at most 0.0055.
Values may be sent and summed in bfloat16 or wider, within the bound.
No kernel may reach another device: no remote copies, remote signals or barrier semaphores. Data moves between devices by JAX's collectives and lax.ppermute only.
A program may use at most 64 MiB of HBM per device.

v0:
```python
import jax
import jax.numpy as jnp
from jax import lax
from jax.sharding import PartitionSpec as P

BATCH = 128


def extended_2(x, sides, width):
    for axis, dim in sides:
        devices, length = (lax.axis_size(axis), x.shape[dim])
        up = [(i, (i + 1) % devices) for i in range(devices - 1)]
        down = [(j, i) for i, j in up]
        last = lax.slice_in_dim(x, length - width, length, axis=dim)
        first = lax.slice_in_dim(x, 0, width, axis=dim)
        before = lax.ppermute(last, axis, up)
        after = lax.ppermute(first, axis, down)
        x = jnp.concatenate([before, x, after], axis=dim)
    return x


def plastic_update(row_block, expand_weight, contract_weight):
    hidden = jax.nn.silu(
        jnp.dot(row_block, expand_weight, preferred_element_type=jnp.float32)
    ).astype(jnp.bfloat16)
    return jnp.dot(hidden, contract_weight, preferred_element_type=jnp.float32).astype(jnp.bfloat16)


def on_device(
    displacement,
    neighbours,
    micro_state,
    strain_loads,
    stiffness,
    expand_weight,
    contract_weight,
    batch_route,
    yield_flags,
    readout,
    external_force,
    coarse_inverse,
):
    extended = extended_2(displacement, (("sub", 2),), 1)
    lower_value = jnp.take(extended[0], neighbours[0], axis=1)
    upper_value = jnp.take(extended[0], neighbours[1], axis=1)
    spacing = (neighbours[1] - neighbours[0]).astype(jnp.float32)
    strain = (upper_value - lower_value) / spacing
    state_rows = micro_state[0]
    row_count = state_rows.shape[0]
    mode_count = state_rows.shape[1]
    per_point = row_count // strain.shape[1]
    per_row = jnp.repeat(strain, per_point, axis=1)
    trial_state = state_rows.astype(jnp.float32) + jnp.dot(
        per_row.T, strain_loads[0], precision=lax.Precision.HIGHEST
    )
    elastic = jnp.dot(
        trial_state.astype(jnp.bfloat16), stiffness[0], preferred_element_type=jnp.float32
    )
    elastic_half = elastic.astype(jnp.bfloat16)
    target = batch_route[0, 0]
    alive_batch = (target >= 0).astype(jnp.int32)
    batch_total = row_count // BATCH
    devices = lax.axis_size("sub")
    reach = min(16, devices // 2, batch_total)
    batches = elastic_half.reshape(batch_total, BATCH, mode_count)
    me = lax.axis_index("sub")
    ahead = (me + jnp.arange(1, reach + 1, dtype=jnp.int32)) % devices
    chosen = (target[None, :] == ahead[:, None]).astype(jnp.bfloat16)
    outgoing = jnp.einsum(
        "db,brm->drm", chosen, batches, preferred_element_type=jnp.float32
    ).astype(jnp.bfloat16)
    updated = plastic_update(
        outgoing.reshape(-1, mode_count), expand_weight[0], contract_weight[0]
    ).reshape(outgoing.shape)
    correction = jnp.einsum(
        "db,drm->brm", chosen, updated, preferred_element_type=jnp.float32
    ).reshape(row_count, mode_count)
    weight_rows = (jnp.repeat(alive_batch, BATCH) * yield_flags[0]).astype(jnp.float32)
    next_state = (elastic + weight_rows[:, None] * correction).astype(jnp.bfloat16)
    projected = jnp.dot(next_state, readout[0], preferred_element_type=jnp.float32)
    averaged = jnp.mean(projected.reshape(-1, per_point), axis=1)
    residual = (external_force[0] - averaged).astype(jnp.bfloat16)[None, :]
    inverse_rows = coarse_inverse[0]
    coarse = jnp.dot(
        inverse_rows,
        lax.all_gather(residual, "sub", axis=1, tiled=True)[0],
        preferred_element_type=jnp.float32,
    )
    return (next_state[None], coarse[None])


def solution(mesh):
    return jax.shard_map(
        on_device,
        mesh=mesh,
        in_specs=(
            P("variant", None, "sub"),
            P(None, "sub"),
            P("variant", "sub", None),
            P("variant", None, None),
            P("variant", None, None),
            P("variant", None, None),
            P("variant", None, None),
            P("variant", None, "sub"),
            P("variant", "sub"),
            P("variant", None),
            P("variant", "sub"),
            P("variant", "sub", None),
        ),
        out_specs=(P("variant", "sub", None), P("variant", "sub")),
        check_vma=False,
    )
```

profile of v0, /device:TPU:0, one launch (start us, length us, event | category | flops | bytes accessed | tf_op | source)
XLA Modules:
  0.0 55.6 jit_solution(13207783952768333148)
XLA Ops:
  0.6 0.0 copy-start
  0.6 0.9 %fusion.45 = (f32[1,6,1]{2,0,1:T(1,128)S(1)}, f32[1,6,1]{2,0,1:T(1,128)S(1)}) fusion(f32[1,6,128]{2,0,1:T(1,128)} %param.14), kind=kLoop, calls=%fused_computation.57 | loop fusion | bytes 96 | tf_op jit(solution)/shard_map/slice | solution.py:14
  1.6 1.3 %collective-permute-start.1 = (f32[1,6,1]{2,0,1:T(1,128)S(1)}, f32[1,6,1]{2,0,1:T(1,128)S(1)}, u32[]{:S(2)}, u32[]{:S(2)}) collective-permute-start(f32[1,6,1]{2,0,1:T(1,128)S(1)} %get-tuple-element.8), channel_id=1, source_target_pairs={{1,0},{2,1},{3,2},{4,3},{5,4},{6,5},{7,6},{9,8},{10,9},{11,10},{12... | collective-permute-start | bytes 80 | tf_op jit(solution)/shard_map/ppermute | solution.py:17
  2.9 3.0 %collective-permute-start = (f32[1,6,1]{2,0,1:T(1,128)S(1)}, f32[1,6,1]{2,0,1:T(1,128)S(1)}, u32[]{:S(2)}, u32[]{:S(2)}) collective-permute-start(f32[1,6,1]{2,0,1:T(1,128)S(1)} %get-tuple-element.7), channel_id=1, source_target_pairs={{0,1},{1,2},{2,3},{3,4},{4,5},{5,6},{6,7},{8,9},{9,10},{10,11},{11... | collective-permute-start | bytes 80 | tf_op jit(solution)/shard_map/ppermute | solution.py:16
  5.9 0.8 %compare_and_fusion.1 = (pred[128]{0:T(512)(128)(4,1)S(1)}, s32[128]{0:T(128)S(1)}, pred[128]{0:T(512)(128)(4,1)S(1)}, s32[128]{0:T(128)S(1)}) fusion(s32[2,128]{1,0:T(2,128)} %param.15), kind=kLoop, calls=%fused_computation.44 | loop fusion | flops 1536 | bytes 2304 | tf_op jit(solution)/shard_map/jit(_take)/and | solution.py:45
  6.7 0.8 %convert_bitcast_fusion = f32[128]{0:T(128)S(1)} fusion(s32[2,128]{1,0:T(2,128)} %param.15), kind=kLoop, calls=%fused_computation.55 | loop fusion | flops 256 | bytes 1536 | tf_op jit(solution)/shard_map/div | solution.py:47
  7.4 0.7 %slice_bitcast_fusion = s32[24]{0:T(128)S(1)} fusion(s32[1,2,24]{2,1,0:T(2,128)} %param.21), kind=kLoop, calls=%fused_computation.54 | loop fusion | bytes 192 | tf_op jit(solution)/shard_map/squeeze | solution.py:60
  8.1 0.7 %compare_convert_fusion = s32[24]{0:T(128)S(1)} fusion(s32[1,2,24]{2,1,0:T(2,128)} %param.21), kind=kLoop, calls=%fused_computation.46 | loop fusion | flops 48 | bytes 192 | tf_op jit(solution)/shard_map/convert_element_type | solution.py:61
  8.8 0.8 %fusion.29 = f32[3072]{0:T(1024)S(1)} fusion(s32[3072]{0:T(1024)} %bitcast.94, s32[24]{0:T(128)S(1)} %compare_convert_fusion), kind=kLoop, calls=%fused_computation.26 | loop fusion | flops 6144 | bytes 24672 | tf_op jit(solution)/shard_map/convert_element_type | solution.py:78
  9.6 0.0 collective-permute-done.1
  9.6 0.0 collective-permute-done
  9.6 0.8 %pad_maximum_fusion = f32[1,6,130]{2,0,1:T(1,128)S(1)} fusion(f32[1,6,1]{2,0,1:T(1,128)S(1)} %collective-permute-done.1, f32[1,6,128]{2,0,1:T(1,128)} %param.14, f32[1,6,1]{2,0,1:T(1,128)S(1)} %collective-permute-done), kind=kLoop, calls=%fused_computation.27 | loop fusion | flops 1560 | bytes 6240 | tf_op jit(solution)/shard_map/concatenate | solution.py:18
  10.4 0.1 copy.41
  10.5 0.6 %gather_fusion.1 = f32[128,6]{1,0:T(8,128)S(1)} fusion(f32[6,130]{0,1:T(8,128)S(1)} %bitcast.92, s32[1024]{0:T(1024)S(1)} %get-tuple-element.13), kind=kCustom, calls=%fused_computation.1.clone | custom fusion | bytes 6656 | tf_op jit(solution)/shard_map/jit(_take)/gather | solution.py:44
  11.1 0.1 copy.43
  11.2 0.7 %gather_fusion = f32[128,6]{1,0:T(8,128)S(1)} fusion(f32[6,130]{0,1:T(8,128)S(1)} %bitcast.93, s32[1024]{0:T(1024)S(1)} %get-tuple-element.14), kind=kCustom, calls=%fused_computation.clone | custom fusion | bytes 6656 | tf_op jit(solution)/shard_map/jit(_take)/gather | solution.py:45
  11.9 0.1 copy.42
  11.9 0.2 broadcast_in_dim.25
  12.1 0.2 reshape.67
  12.4 0.0 copy-start.2
  12.4 7.1 %fusion = bf16[3072,512]{1,0:T(8,128)(2,1)S(1)} fusion(f32[6,3072]{1,0:T(8,128)S(1)} %reshape.67, bf16[1,3072,512]{2,1,0:T(8,128)(2,1)} %param.16, f32[1,6,512]{2,0,1:T(1,128)} %param.17), kind=kOutput, calls=%fused_computation.3 | convolution fusion | flops 117964800 | bytes 6377472 | tf_op jit(solution)/shard_map/dot_general | solution.py:53
  19.5 0.0 copy-done.2
  19.5 4.4 %fusion.46 = (bf16[3072,512]{1,0:T(8,128)(2,1)S(1)}, f32[3072,512]{1,0:T(8,128)}) fusion(bf16[3072,512]{1,0:T(8,128)(2,1)S(1)} %fusion, bf16[1,512,512]{2,1,0:T(8,128)(2,1)S(1)} %copy-done.2), kind=kOutput, calls=%fused_computation.58 | convolution fusion | flops 1612185600 | bytes 13107200 | tf_op jit(solution)/shard_map/dot_general | solution.py:56
  23.9 2.3 %fusion.18 = bf16[4,128,512]{2,0,1:T(4,128)(2,1)S(1)} fusion(bf16[24,128,512]{2,1,0:T(8,128)(2,1)S(1)} %bitcast.87, s32[24]{0:T(128)S(1)} %slice_bitcast_fusion, s32[4]{0:T(128)S(1)} %and_select_fusion), kind=kOutput, calls=%fused_computation.15 | convolution fusion | flops 12845152 | bytes 3670128 | tf_op jit(solution)/shard_map/db,brm->drm/dot_general | solution.py:69
  26.2 0.1 copy.45
  26.3 0.0 copy-done
  26.3 4.3 %fusion.13 = bf16[512,512]{1,0:T(8,128)(2,1)S(1)} fusion(bf16[1,2048,512]{2,1,0:T(8,128)(2,1)S(1)} %copy-done, bf16[512,512]{1,0:T(8,128)(2,1)S(1)} %bitcast.91, bf16[1,512,2048]{2,1,0:T(8,128)(2,1)} %param.19), kind=kOutput, calls=%fused_computation.14 | convolution fusion | flops 2152988672 | bytes 5242880 | tf_op jit(solution)/shard_map/dot_general | solution.py:26
  30.6 0.0 slice-start
  30.6 1.1 %fusion.23 = f32[24,128,512]{2,0,1:T(8,128)S(1)} fusion(bf16[4,128,512]{2,1,0:T(8,128)(2,1)S(1)} %bitcast.90, s32[24]{0:T(128)S(1)} %slice_bitcast_fusion, s32[4]{0:T(128)S(1)} %and_select_fusion), kind=kOutput, calls=%fused_computation.18 | convolution fusion | flops 12583008 | bytes 6815856 | tf_op jit(solution)/shard_map/db,drm->brm/dot_general | solution.py:75
  31.8 0.0 slice-start.1
  31.8 3.6 %copy.47 = f32[24,128,512]{2,1,0:T(8,128)S(1)} copy(f32[24,128,512]{2,0,1:T(8,128)S(1)} %fusion.23) | data formatting | bytes 12582912 | tf_op jit(solution)/shard_map/db,drm->brm/dot_general | solution.py:75
  35.4 0.0 slice-done
  35.4 0.0 slice-done.1
  35.4 0.0 copy-start.4
  35.5 1.4 %fusion.2 = bf16[3072,512]{1,0:T(8,128)(2,1)S(1)} fusion(f32[3072,512]{1,0:T(8,128)S(1)} %bitcast.86, f32[24,128,512]{2,1,0:T(8,128)S(1)} %copy.47, f32[3072]{0:T(1024)S(1)} %fusion.29), kind=kLoop, calls=%fused_computation.6 | loop fusion | flops 4718592 | bytes 15740928 | tf_op jit(solution)/shard_map/convert_element_type | solution.py:79
  36.9 0.0 copy-start.1
  36.9 0.0 copy-start.5
  36.9 0.0 copy-start.3
  36.9 1.6 %copy-done.1 = bf16[3072,512]{1,0:T(8,128)(2,1)} copy-done((bf16[3072,512]{1,0:T(8,128)(2,1)}, bf16[3072,512]{1,0:T(8,128)(2,1)S(1)}, u32[]{:S(2)}) %copy-start.1) | copy-done | bytes 3145752
  38.5 0.0 copy-done.4
  38.6 2.8 %fusion.32 = f32[1,128,24]{2,0,1:T(1,128)S(1)} fusion(bf16[128,24,512]{2,1,0:T(8,128)(2,1)S(1)} %bitcast.88, bf16[1,512]{1,0:T(2,128)(2,1)S(1)} %copy-done.4), kind=kOutput, calls=%fused_computation.37 | convolution fusion | flops 3145728 | bytes 3159040 | tf_op jit(solution)/shard_map/dot_general | solution.py:80
  41.4 0.1 copy.48
  41.5 0.0 copy-done.5
  41.5 13.4 %all_gather.3 = bf16[1,1024]{1,0:T(2,128)(2,1)S(1)} all-gather(bf16[1,128]{1,0:T(2,128)(2,1)S(1)} %fusion.43), channel_id=1, replica_groups=mesh['variant'=4,'sub'=8] {'sub'}, dimensions={1}, use_global_device_ids=true | all-gather | bytes 2304 | tf_op jit(solution)/shard_map/all_gather | solution.py:86
  54.9 0.0 copy-done.3
  54.9 0.7 %fusion.25 = f32[1,128]{1,0:T(1,128)} fusion(bf16[1,128,1024]{2,1,0:T(8,128)(2,1)S(1)} %copy-done.3, bf16[1,1024]{1,0:T(2,128)(2,1)S(1)} %all_gather.3), kind=kOutput, calls=%fused_computation.20 | convolution fusion | flops 262144 | bytes 264704 | tf_op jit(solution)/shard_map/dot_general | solution.py:84
  (6 shorter events, 0.1 us)
Async XLA Ops:
  0.6 25.7 %copy-start = (bf16[1,2048,512]{2,1,0:T(8,128)(2,1)S(1)}, bf16[1,2048,512]{2,1,0:T(8,128)(2,1)}, u32[]{:S(2)}) copy-start(bf16[1,2048,512]{2,1,0:T(8,128)(2,1)} %param.20) | copy-start | bytes 6291460
  1.6 8.0 %collective-permute-start.1 = (f32[1,6,1]{2,0,1:T(1,128)S(1)}, f32[1,6,1]{2,0,1:T(1,128)S(1)}, u32[]{:S(2)}, u32[]{:S(2)}) collective-permute-start(f32[1,6,1]{2,0,1:T(1,128)S(1)} %get-tuple-element.8), channel_id=1, source_target_pairs={{1,0},{2,1},{3,2},{4,3},{5,4},{6,5},{7,6},{9,8},{10,9},{11,10},{12... | collective-permute-start | bytes 80 | tf_op jit(solution)/shard_map/ppermute | solution.py:17
  2.9 6.7 %collective-permute-start = (f32[1,6,1]{2,0,1:T(1,128)S(1)}, f32[1,6,1]{2,0,1:T(1,128)S(1)}, u32[]{:S(2)}, u32[]{:S(2)}) collective-permute-start(f32[1,6,1]{2,0,1:T(1,128)S(1)} %get-tuple-element.7), channel_id=1, source_target_pairs={{0,1},{1,2},{2,3},{3,4},{4,5},{5,6},{6,7},{8,9},{9,10},{10,11},{11... | collective-permute-start | bytes 80 | tf_op jit(solution)/shard_map/ppermute | solution.py:16
  12.4 7.1 %copy-start.2 = (bf16[1,512,512]{2,1,0:T(8,128)(2,1)S(1)}, bf16[1,512,512]{2,1,0:T(8,128)(2,1)}, u32[]{:S(2)}) copy-start(bf16[1,512,512]{2,1,0:T(8,128)(2,1)} %param.18) | copy-start | bytes 1572868
  30.6 4.8 %slice-start = ((s8[6291456]{0:T(1024)(128)(4,1)}), s8[4194304]{0:T(1024)(128)(4,1)S(1)}, s32[]{:S(2)}) async-start(s8[6291456]{0:T(1024)(128)(4,1)} %bitcast.85), calls=%async_computation | async-start | bytes 8388608
  31.8 3.7 %slice-start.1 = ((s8[6291456]{0:T(1024)(128)(4,1)}), s8[2097152]{0:T(1024)(128)(4,1)S(1)}, s32[]{:S(2)}) async-start(s8[6291456]{0:T(1024)(128)(4,1)} %bitcast.85), calls=%async_computation.1 | async-start | bytes 4194304
  35.4 3.1 %copy-start.4 = (bf16[1,512]{1,0:T(2,128)(2,1)S(1)}, bf16[1,512]{1,0:T(2,128)(2,1)}, u32[]{:S(2)}) copy-start(bf16[1,512]{1,0:T(2,128)(2,1)} %param.23) | copy-start | bytes 3076
  36.9 1.7 %copy-start.1 = (bf16[3072,512]{1,0:T(8,128)(2,1)}, bf16[3072,512]{1,0:T(8,128)(2,1)S(1)}, u32[]{:S(2)}) copy-start(bf16[3072,512]{1,0:T(8,128)(2,1)S(1)} %fusion.2) | copy-start | bytes 9437188
  36.9 4.6 %copy-start.5 = (f32[1,128]{1,0:T(1,128)S(1)}, f32[1,128]{1,0:T(1,128)}, u32[]{:S(2)}) copy-start(f32[1,128]{1,0:T(1,128)} %param.24) | copy-start | bytes 1540
  36.9 18.0 %copy-start.3 = (bf16[1,128,1024]{2,1,0:T(8,128)(2,1)S(1)}, bf16[1,128,1024]{2,1,0:T(8,128)(2,1)}, u32[]{:S(2)}) copy-start(bf16[1,128,1024]{2,1,0:T(8,128)(2,1)} %param.25) | copy-start | bytes 786436
where the time goes:
time: 55.9 us; the launch traced here: 55.6 us
  matrix products  22.7 us (41%)
  blocking collectives  13.4 us (24%)
  local copies, waits for them, and re-layouts  9.03 us (16%)
  other arithmetic  5.24 us (9%)
  starting transfers between devices  4.31 us (8%)
  between operations  0.86 us (2%)
    all_gather x1, blocking collectives, on_device(): lax.all_gather(residual, 'sub', axis=1, tiled=True)[0]  13.4 us
    dot_general x1, matrix products, on_device(): jnp.dot(per_row.T, strain_loads[0], precision=lax.Precision.HIGHEST)  7.11 us
    dot_general x1, matrix products, on_device(): jnp.dot(trial_state.astype(jnp.bfloat16), stiffness[0], preferred_element...  4.45 us
    dot_general x1, matrix products, plastic_update(): jnp.dot(hidden, contract_weight, preferred_element_type=jnp.float32)  4.27 us
    dot_general x1, local copies, waits for them, and re-layouts, on_device(): jnp.einsum('db,drm->brm', chosen, updated, preferred_element_type=jnp.flo...  3.64 us
    ppermute x1, starting transfers between devices, extended_2(): before = lax.ppermute(last, axis, up)  3.03 us
    dot_general x1, matrix products, on_device(): jnp.dot(next_state, readout[0], preferred_element_type=jnp.float32)  2.81 us
    dot_general x1, matrix products, on_device(): jnp.einsum('db,brm->drm', chosen, batches, preferred_element_type=jnp.flo...  2.29 us
  transfers between devices with their start and end apart: 2, of which 0 were waited for; matrix products, arithmetic and copies ran while one was open for 7% of the time, Pallas kernels for 0%

commit v1 on v0

v1 whole, which is shorter than its diff:
```python
import functools

import jax
import jax.numpy as jnp
from jax import lax
from jax.experimental import pallas as pl
from jax.experimental.pallas import tpu as pltpu
from jax.sharding import PartitionSpec as P

BATCH = 128
GROUP = 8
TILE = 32
MIB = 1 << 20
F32 = jnp.float32
BF16 = jnp.bfloat16
NT = (((1,), (1,)), ((), ()))


def dot(a, b):
    return jnp.dot(a, b, preferred_element_type=F32)


def dot_nt(a, b, precision=None):
    return lax.dot_general(a, b, NT, precision=precision, preferred_element_type=F32)


def halves(x):
    high = x.astype(BF16)
    return high, (x - high.astype(F32)).astype(BF16)


def silu(a):
    half = 0.5 * a
    return half + half * jnp.tanh(half)


def list_alive(route_ref, list_ref, batches):
    count = jnp.int32(0)
    for b in range(batches):
        list_ref[count] = jnp.int32(b)
        count = count + (route_ref[0, 0, b] >= 0).astype(jnp.int32)
    return count


def step_kernel(
    per_point,
    width,
    core_ref,
    chip_ref,
    pick_ref,
    *refs,
):
    sources, outs, rest = refs[:11], refs[11:13], refs[13:]
    held_refs = sources
    route_ref, displacement_ref, neighbours_ref, loads_ref, readout_ref, force_ref, flags_ref = held_refs[:7]
    state_ref, stiffness_ref, expand_ref, contract_ref = held_refs[7:]
    out_ref, residual_ref = outs
    list_ref, next_ref, hidden_ref, point_ref, sum_ref, out_sems, batch_sems = rest
    points = displacement_ref.shape[2]
    rows, modes = state_ref.shape[1:]
    batches = rows // BATCH
    tile_points = TILE
    tile = tile_points * per_point
    tiles = points // tile_points
    spans = [slice(t * tile, (t + 1) * tile) for t in range(tiles)]

    count = list_alive(route_ref, list_ref, batches)

    odd = lax.axis_index("sub") % 2 == 1
    own, core, chip = (
        jnp.concatenate([ref[k] for k in range(ref.shape[0])], axis=0)
        for ref in (displacement_ref, core_ref, chip_ref)
    )
    before = jnp.where(odd, core, chip)
    after = jnp.where(odd, chip, core)
    place = lax.broadcasted_iota(jnp.int32, own.shape, 1)
    left = jnp.where(place == 0, pltpu.roll(before, 1, 1), pltpu.roll(own, 1, 1))
    right = jnp.where(
        place == points - 1, pltpu.roll(after, points - 1, 1), pltpu.roll(own, points - 1, 1)
    )
    first, second = neighbours_ref[0:1, :], neighbours_ref[1:2, :]
    lower = jnp.where(first == place, left, own)
    upper = jnp.where(second == place + 2, right, own)
    strain = (upper - lower) / (second - first).astype(F32)
    loads = jnp.concatenate([loads_ref[k] for k in range(loads_ref.shape[0])], axis=0)
    load = lax.dot_general(
        strain,
        loads,
        (((0,), (0,)), ((), ())),
        precision=lax.Precision.HIGHEST,
        preferred_element_type=F32,
    )
    stiffness = stiffness_ref[0]
    shift = dot(jnp.concatenate(halves(load), axis=0), stiffness)
    point_ref[...] = shift[:points, :] + shift[points:, :]

    outgoing = [
        pltpu.make_async_copy(next_ref.at[s, :], out_ref.at[0, s, :], out_sems.at[t])
        for t, s in enumerate(spans)
    ]
    for t, span in enumerate(spans):
        acc = dot(state_ref[0, span, :], stiffness)
        shift = point_ref[t * tile_points : (t + 1) * tile_points, :]
        acc = acc.reshape(tile_points, per_point, modes) + shift[:, None, :]
        next_ref[span, :] = acc.reshape(tile, modes).astype(BF16)
        outgoing[t].start()
    for copy in outgoing:
        copy.wait()

    @pl.loop(0, (count + width - 1) // width)
    def _(c):
        chosen = [list_ref[jnp.minimum(c * width + j, count - 1)] for j in range(width)]
        starts = [pl.multiple_of(b * BATCH, BATCH) for b in chosen]
        taken = jnp.concatenate([next_ref[pl.ds(s, BATCH), :] for s in starts], axis=0)
        for h in range(0, expand_ref.shape[2], 512):
            hidden_ref[:, h : h + 512] = silu(dot(taken, expand_ref[0, :, h : h + 512])).astype(BF16)
        correction = dot(hidden_ref[...], contract_ref[0])
        for j, s in enumerate(starts):
            at = slice(j * BATCH, (j + 1) * BATCH)
            flags = flags_ref[0:1, pl.ds(s, BATCH)].astype(F32)
            column = jnp.broadcast_to(flags, (BATCH, BATCH)).T
            column = jnp.concatenate([column] * (modes // BATCH), axis=1)
            next_ref[pl.ds(s, BATCH), :] = (taken[at, :].astype(F32) + column * correction[at, :]).astype(BF16)

    def changed(i):
        s = pl.multiple_of(list_ref[i] * BATCH, BATCH)
        span = pl.ds(s, BATCH)
        return pltpu.make_async_copy(next_ref.at[span, :], out_ref.at[0, span, :], batch_sems)

    @pl.loop(0, count)
    def _(i):
        changed(i).start()

    for t, span in enumerate(spans):
        sum_ref[t * tile_points : (t + 1) * tile_points, :] = dot(pick_ref[...], next_ref[span, :])
    readout = jnp.broadcast_to(readout_ref[...], (GROUP, modes)).astype(F32)
    mean = dot_nt(readout, sum_ref[...], lax.Precision.HIGHEST)[0:1, :] * (1.0 / per_point)
    residual_ref[...] = (force_ref[...] - mean).astype(BF16)

    @pl.loop(0, count)
    def _(i):
        changed(i).wait()


def pick_kernel(per_point, pick_ref):
    shape = pick_ref.shape
    p = lax.broadcasted_iota(jnp.int32, shape, 0)
    r = lax.broadcasted_iota(jnp.int32, shape, 1)
    pick_ref[...] = jnp.where((r >= p * per_point) & (r < (p + 1) * per_point), 1.0, 0.0).astype(BF16)


def coarse_kernel(inverse_ref, *refs):
    pairs, out_ref = refs[:-1], refs[-1]
    points = out_ref.shape[1]
    me = lax.axis_index("sub")
    total = jnp.zeros((GROUP, points), F32)
    for k, pair_ref in enumerate(pairs):
        chip = (me // 2) ^ k
        for c in range(2):
            block = pl.multiple_of((2 * chip + (me + c) % 2) * points, points)
            part = jnp.broadcast_to(pair_ref[c : c + 1, :], (GROUP, points))
            total = total + dot_nt(part, inverse_ref[0, :, pl.ds(block, points)])
    out_ref[...] = total[0:1, :]


def swap_pairs(n, offset):
    pairs = [(i, i + 1) for i in range(offset, n - 1, 2)]
    return pairs + [(j, i) for i, j in pairs]


def on_device(
    displacement,
    neighbours,
    micro_state,
    strain_loads,
    stiffness,
    expand_weight,
    contract_weight,
    batch_route,
    yield_flags,
    readout,
    external_force,
    coarse_inverse,
):
    n = lax.axis_size("sub")
    points = displacement.shape[2]
    rows, modes = micro_state.shape[1:]
    hidden_size = expand_weight.shape[2]
    per_point = rows // points
    batches = rows // BATCH
    width = min(4, n // 2, batches)
    field = jnp.transpose(displacement, (1, 0, 2))
    vmem = pl.BlockSpec(memory_space=pltpu.VMEM)
    pick = pl.pallas_call(
        functools.partial(pick_kernel, per_point),
        out_shape=jax.ShapeDtypeStruct((TILE, TILE * per_point), BF16),
        out_specs=vmem,
        compiler_params=pltpu.CompilerParams(vmem_limit_bytes=MIB),
        cost_estimate=pl.CostEstimate(flops=20 * 10**9, bytes_accessed=MIB, transcendentals=0),
    )()
    loads = jnp.transpose(strain_loads, (1, 0, 2))
    from_core = lax.ppermute(field, "sub", swap_pairs(n, 0))
    from_chip = lax.ppermute(field, "sub", swap_pairs(n, 1))
    hbm = pl.BlockSpec(memory_space=pltpu.HBM)
    sources = (
        batch_route,
        field,
        neighbours,
        loads,
        readout,
        external_force,
        yield_flags,
        micro_state,
        stiffness,
        expand_weight,
        contract_weight,
    )
    tiles = points // TILE
    states_next, residual = pl.pallas_call(
        functools.partial(step_kernel, per_point, width),
        out_shape=(
            jax.ShapeDtypeStruct((1, rows, modes), BF16),
            jax.ShapeDtypeStruct((1, points), BF16),
        ),
        in_specs=[vmem] * 3 + [pl.BlockSpec(memory_space=pltpu.SMEM)] + [vmem] * (len(sources)-1),
        out_specs=(hbm, vmem),
        scratch_shapes=[
            pltpu.SMEM((batches + 1,), jnp.int32),
            pltpu.VMEM((rows, modes), BF16),
            pltpu.VMEM((width * BATCH, hidden_size), BF16),
            pltpu.VMEM((points, modes), F32),
            pltpu.VMEM((points, modes), F32),
            pltpu.SemaphoreType.DMA((tiles,)),
            pltpu.SemaphoreType.DMA(()),
        ],
        compiler_params=pltpu.CompilerParams(vmem_limit_bytes=24 * MIB),
        cost_estimate=pl.CostEstimate(
            flops=2 * rows * modes * modes + 4 * width * BATCH * modes * hidden_size,
            bytes_accessed=11 * MIB,
            transcendentals=0,
        ),
    )(from_core, from_chip, pick, *sources)
    other = lax.ppermute(residual, "sub", swap_pairs(n, 0))
    pair = jnp.concatenate([residual, other], axis=0)
    pairs = [pair] + [
        lax.ppermute(pair, "sub", [(i, i ^ (2 * k)) for i in range(n)]) for k in range(1, n // 2)
    ]
    coarse = pl.pallas_call(
        coarse_kernel,
        out_shape=jax.ShapeDtypeStruct((1, points), F32),
        in_specs=[vmem] * (1 + len(pairs)),
        out_specs=vmem,
        compiler_params=pltpu.CompilerParams(vmem_limit_bytes=4 * MIB),
    )(coarse_inverse, *pairs)
    return (states_next, coarse)


def solution(mesh):
    return jax.shard_map(
        on_device,
        mesh=mesh,
        in_specs=(
            P("variant", None, "sub"),
            P(None, "sub"),
            P("variant", "sub", None),
            P("variant", None, None),
            P("variant", None, None),
            P("variant", None, None),
            P("variant", None, None),
            P("variant", None, "sub"),
            P("variant", "sub"),
            P("variant", None),
            P("variant", "sub"),
            P("variant", "sub", None),
        ),
        out_specs=(P("variant", "sub", None), P("variant", "sub")),
        check_vma=False,
    )
```

time: 55.9 us -> 25.5 us (0.46)
  matrix products: 22.7 us -> 0 us
  blocking collectives: 13.4 us -> 0 us
  local copies, waits for them, and re-layouts: 9.03 us -> 0.05 us
  starting transfers between devices: 4.31 us -> 13.1 us
  Pallas kernels: 0 us -> 5.72 us
  waiting for transfers between devices: 0.01 us -> 5.62 us
  other arithmetic: 5.24 us -> 0.01 us
    dot_general x7 -> x0, matrix products: 22.7 us -> none  [the longest x1 7.11 us: on_device(): jnp.dot(per_row.T, strain_loads[0], precision=lax.Precision.HIGHEST)]
    all_gather x1 -> x0, blocking collectives: 13.4 us -> none  [on_device(): lax.all_gather(residual, 'sub', axis=1, tiled=True)[0]]
    ppermute x2 -> x6, starting transfers between devices: 4.31 us -> 13.1 us  [the longest x1 4.58 us: on_device(): from_core = lax.ppermute(field, 'sub', swap_pairs(n, 0))]
    pallas_call x0 -> x3, Pallas kernels: none -> 5.72 us  [the longest x1 4.92 us: on_device(): pl.pallas_call(functools.partial(step_kernel, per_point, width), out_shap...]
    ppermute x2 -> x6, waiting for transfers between devices: 0.01 us -> 5.62 us  [the longest x3 3.8 us: on_device(): lax.ppermute(pair, 'sub', [(i, i ^ 2 * k) for i in range(n)])]
    dot_general x2 -> x0, local copies, waits for them, and re-layouts: 3.71 us -> none  [the longest x1 3.64 us: on_device(): jnp.einsum('db,drm->brm', chosen, updated, preferred_element_type=jnp.flo...]
    convert_element_type x4 -> x0, other arithmetic: 2.89 us -> none  [the longest x1 1.42 us: on_device(): (elastic + weight_rows[:, None] * correction).astype(jnp.bfloat16)]
    unnamed x16 -> x24, local copies, waits for them, and re-layouts: 1.68 us -> 0.05 us
  transfers between devices with their start and end apart: 2 -> 6, of which waited for: 0 -> 4; matrix products, arithmetic and copies ran while one was open for 7% -> 0% of each run, Pallas kernels for 0% -> 0%
where the time goes in v1:
time: 25.5 us; the launch traced here: 25.4 us
  starting transfers between devices  13.1 us (51%)
  Pallas kernels  5.72 us (22%)
  waiting for transfers between devices  5.62 us (22%)
  between operations  0.82 us (3%)
    pallas_call x1, Pallas kernels, on_device(): pl.pallas_call(functools.partial(step_kernel, per_point, width), out_shap...  4.92 us
    ppermute x1, starting transfers between devices, on_device(): from_core = lax.ppermute(field, 'sub', swap_pairs(n, 0))  4.58 us
    ppermute x3, starting transfers between devices, on_device(): lax.ppermute(pair, 'sub', [(i, i ^ 2 * k) for i in range(n)])  4.5 us
    ppermute x3, waiting for transfers between devices, on_device(): lax.ppermute(pair, 'sub', [(i, i ^ 2 * k) for i in range(n)])  3.8 us
    ppermute x1, starting transfers between devices, on_device(): other = lax.ppermute(residual, 'sub', swap_pairs(n, 0))  3.26 us
    ppermute x1, waiting for transfers between devices, on_device(): from_core = lax.ppermute(field, 'sub', swap_pairs(n, 0))  1 us
    ppermute x1, waiting for transfers between devices, on_device(): other = lax.ppermute(residual, 'sub', swap_pairs(n, 0))  0.82 us
    ppermute x1, starting transfers between devices, on_device(): from_chip = lax.ppermute(field, 'sub', swap_pairs(n, 1))  0.79 us
  transfers between devices with their start and end apart: 6, of which 4 were waited for; matrix products, arithmetic and copies ran while one was open for 0% of the time, Pallas kernels for 0%

profile of v1, /device:TPU:0, one launch (start us, length us, event | category | flops | bytes accessed | tf_op | source)
XLA Modules:
  0.0 25.4 jit_solution(14765935414180665464)
XLA Ops:
  0.6 0.0 copy-start.1
  0.6 0.0 copy-start.2
  0.7 0.0 copy-start.3
  0.7 0.0 copy-start.4
  0.7 0.0 copy-start.5
  0.7 0.0 copy-start.6
  0.7 0.0 copy-start.7
  0.7 0.0 copy-start.8
  0.7 0.0 copy-start.9
  0.7 0.0 copy-start.10
  0.7 0.0 copy-start.11
  0.7 0.8 %collective-permute-start.1 = (f32[6,1,128]{2,1,0:T(1,128)}, f32[6,1,128]{2,1,0:T(1,128)S(1)}, u32[]{:S(2)}, u32[]{:S(2)}) collective-permute-start(f32[6,1,128]{2,1,0:T(1,128)} %bitcast.3), channel_id=1, source_target_pairs={{1,2},{3,4},{5,6},{2,1},{4,3},{6,5},{9,10},{11,12},{13,14},{10,9},... | collective-permute-start | bytes 9224 | tf_op jit(solution)/shard_map/ppermute | solution.py:203
  1.5 4.6 %collective-permute-start = (f32[6,1,128]{2,1,0:T(1,128)}, f32[6,1,128]{2,1,0:T(1,128)S(1)}, u32[]{:S(2)}, u32[]{:S(2)}) collective-permute-start(f32[6,1,128]{2,1,0:T(1,128)} %bitcast.4), channel_id=1, source_target_pairs={{0,1},{2,3},{4,5},{6,7},{1,0},{3,2},{5,4},{7,6},{8,9},{10,11},{12,... | collective-permute-start | bytes 9224 | tf_op jit(solution)/shard_map/ppermute | solution.py:202
  6.2 0.0 collective-permute-done.1.chip_ref
  6.2 1.0 %collective-permute-done.core_ref = f32[6,1,128]{2,1,0:T(1,128)S(1)} collective-permute-done((f32[6,1,128]{2,1,0:T(1,128)}, f32[6,1,128]{2,1,0:T(1,128)S(1)}, u32[]{:S(2)}, u32[]{:S(2)}) %collective-permute-start) | collective-permute-done | bytes 3104 | tf_op jit(solution)/shard_map/ppermute | solution.py:202
  7.2 0.0 copy-done.1
  7.2 0.0 copy-done.2
  7.2 0.0 copy-done.3
  7.2 0.0 copy-done.4
  7.2 0.0 copy-done.5
  7.2 0.0 copy-done.6
  7.2 0.0 copy-done.7
  7.2 0.0 copy-done.8
  7.2 0.0 copy-done.9
  7.2 0.0 copy-done.10
  7.2 0.0 copy-done.11
  7.2 0.0 copy-start
  7.3 4.9 %shard_map.132 = (bf16[1,3072,512]{2,1,0:T(8,128)(2,1)}, bf16[1,128]{1,0:T(2,128)(2,1)S(1)}) custom-call(f32[6,1,128]{2,1,0:T(1,128)S(1)} %collective-permute-done.core_ref, f32[6,1,128]{2,1,0:T(1,128)S(1)} %collective-permute-done.1.chip_ref, bf16[32,768]{1,0:T(8,128)(2,1)S(1)} %shard_map.131.pick_ref, s32[1,2,24]{2,1,0:T(2,128)S(1)} %copy-done.9, ...), custom_call_target="tpu_custom_call" | custom-call | flops 3758096384 | bytes 11534336 | tf_op jit(solution)/shard_map/pallas_call | solution.py:219
  12.2 3.3 %collective-permute-start.2 = (bf16[1,128]{1,0:T(2,128)(2,1)S(1)}, bf16[1,128]{1,0:T(2,128)(2,1)S(1)}, u32[]{:S(2)}, u32[]{:S(2)}) collective-permute-start(bf16[1,128]{1,0:T(2,128)(2,1)S(1)} %get-tuple-element.5), channel_id=1, source_target_pairs={{0,1},{2,3},{4,5},{6,7},{1,0},{3,2},{5,4},{7,6},{8,9},{10,11},{12,... | collective-permute-start | bytes 776 | tf_op jit(solution)/shard_map/ppermute | solution.py:243
  15.4 0.8 %collective-permute-done.2 = bf16[1,128]{1,0:T(2,128)(2,1)S(1)} collective-permute-done((bf16[1,128]{1,0:T(2,128)(2,1)S(1)}, bf16[1,128]{1,0:T(2,128)(2,1)S(1)}, u32[]{:S(2)}, u32[]{:S(2)}) %collective-permute-start.2) | collective-permute-done | bytes 288 | tf_op jit(solution)/shard_map/ppermute | solution.py:243
  16.3 3.9 %collective-permute-start.5 = (bf16[2,128]{1,0:T(2,128)(2,1)S(1)}, bf16[2,128]{1,0:T(2,128)(2,1)S(1)}, u32[]{:S(2)}, u32[]{:S(2)}) collective-permute-start(bf16[2,128]{1,0:T(2,128)(2,1)S(1)} %pad_maximum_fusion.refs_0_), channel_id=1, source_target_pairs={{0,6},{1,7},{2,4},{3,5},{4,2},{5,3},{6,0},{7,1},{8,14},{9,15},{10,... | collective-permute-start | bytes 1544 | tf_op jit(solution)/shard_map/ppermute | solution.py:246
  20.1 0.0 collective-permute-start.4
  20.1 0.6 %collective-permute-start.3 = (bf16[2,128]{1,0:T(2,128)(2,1)S(1)}, bf16[2,128]{1,0:T(2,128)(2,1)S(1)}, u32[]{:S(2)}, u32[]{:S(2)}) collective-permute-start(bf16[2,128]{1,0:T(2,128)(2,1)S(1)} %pad_maximum_fusion.refs_0_), channel_id=1, source_target_pairs={{0,2},{1,3},{2,0},{3,1},{4,6},{5,7},{6,4},{7,5},{8,10},{9,11},{10,... | collective-permute-start | bytes 1544 | tf_op jit(solution)/shard_map/ppermute | solution.py:246
  20.8 0.9 %collective-permute-done.5.refs_3_ = bf16[2,128]{1,0:T(2,128)(2,1)S(1)} collective-permute-done((bf16[2,128]{1,0:T(2,128)(2,1)S(1)}, bf16[2,128]{1,0:T(2,128)(2,1)S(1)}, u32[]{:S(2)}, u32[]{:S(2)}) %collective-permute-start.5) | collective-permute-done | bytes 544 | tf_op jit(solution)/shard_map/ppermute | solution.py:246
  21.7 2.9 %collective-permute-done.4.refs_2_ = bf16[2,128]{1,0:T(2,128)(2,1)S(1)} collective-permute-done((bf16[2,128]{1,0:T(2,128)(2,1)S(1)}, bf16[2,128]{1,0:T(2,128)(2,1)S(1)}, u32[]{:S(2)}, u32[]{:S(2)}) %collective-permute-start.4) | collective-permute-done | bytes 544 | tf_op jit(solution)/shard_map/ppermute | solution.py:246
  24.6 0.0 collective-permute-done.3.refs_1_
  24.6 0.0 copy-done
  24.6 0.8 %shard_map.133 = f32[1,128]{1,0:T(1,128)} custom-call(bf16[1,128,1024]{2,1,0:T(8,128)(2,1)S(1)} %copy-done, bf16[2,128]{1,0:T(2,128)(2,1)S(1)} %pad_maximum_fusion.refs_0_, bf16[2,128]{1,0:T(2,128)(2,1)S(1)} %collective-permute-done.3.refs_1_, bf16[2,128]{1,0:T(2,128)(2,1)S(1)} %collective-permute-done.4.refs_2_, ...), custom_call_target="tpu_custom_call" | custom-call | tf_op jit(solution)/shard_map/pallas_call | solution.py:248
  (2 shorter events, 0.0 us)
Async XLA Ops:
  0.6 6.5 %copy-start.1 = (bf16[1,3072,512]{2,1,0:T(8,128)(2,1)S(1)}, bf16[1,3072,512]{2,1,0:T(8,128)(2,1)}, u32[]{:S(2)}) copy-start(bf16[1,3072,512]{2,1,0:T(8,128)(2,1)} %refs_7_.1) | copy-start | bytes 9437188
  0.6 6.5 %copy-start.2 = (bf16[1,512,2048]{2,1,0:T(8,128)(2,1)S(1)}, bf16[1,512,2048]{2,1,0:T(8,128)(2,1)}, u32[]{:S(2)}) copy-start(bf16[1,512,2048]{2,1,0:T(8,128)(2,1)} %refs_9_.1) | copy-start | bytes 6291460
  0.7 6.5 %copy-start.3 = (bf16[1,2048,512]{2,1,0:T(8,128)(2,1)S(1)}, bf16[1,2048,512]{2,1,0:T(8,128)(2,1)}, u32[]{:S(2)}) copy-start(bf16[1,2048,512]{2,1,0:T(8,128)(2,1)} %refs_10_.1) | copy-start | bytes 6291460
  0.7 6.5 %copy-start.4 = (bf16[1,512,512]{2,1,0:T(8,128)(2,1)S(1)}, bf16[1,512,512]{2,1,0:T(8,128)(2,1)}, u32[]{:S(2)}) copy-start(bf16[1,512,512]{2,1,0:T(8,128)(2,1)} %refs_8_.1) | copy-start | bytes 1572868
  0.7 6.5 %copy-start.5 = (f32[1,6,512]{2,0,1:T(1,128)S(1)}, f32[1,6,512]{2,0,1:T(1,128)}, u32[]{:S(2)}) copy-start(f32[1,6,512]{2,0,1:T(1,128)} %param.15) | copy-start | bytes 36868
  0.7 6.5 %copy-start.6 = (s32[1,3072]{1,0:T(1,128)S(1)}, s32[1,3072]{1,0:T(1,128)}, u32[]{:S(2)}) copy-start(s32[1,3072]{1,0:T(1,128)} %refs_6_.1) | copy-start | bytes 36868
  0.7 6.5 %copy-start.7 = (f32[1,6,128]{2,0,1:T(1,128)S(1)}, f32[1,6,128]{2,0,1:T(1,128)}, u32[]{:S(2)}) copy-start(f32[1,6,128]{2,0,1:T(1,128)} %param.12) | copy-start | bytes 9220
  0.7 6.5 %copy-start.8 = (bf16[1,512]{1,0:T(2,128)(2,1)S(1)}, bf16[1,512]{1,0:T(2,128)(2,1)}, u32[]{:S(2)}) copy-start(bf16[1,512]{1,0:T(2,128)(2,1)} %refs_4_.1) | copy-start | bytes 3076
  0.7 6.5 %copy-start.9 = (s32[1,2,24]{2,1,0:T(2,128)S(1)}, s32[1,2,24]{2,1,0:T(2,128)}, u32[]{:S(2)}) copy-start(s32[1,2,24]{2,1,0:T(2,128)} %refs_0_.1) | copy-start | bytes 580
  0.7 6.5 %copy-start.10 = (s32[2,128]{1,0:T(2,128)S(1)}, s32[2,128]{1,0:T(2,128)}, u32[]{:S(2)}) copy-start(s32[2,128]{1,0:T(2,128)} %refs_2_.1) | copy-start | bytes 3076
  0.7 6.5 %copy-start.11 = (f32[1,128]{1,0:T(1,128)S(1)}, f32[1,128]{1,0:T(1,128)}, u32[]{:S(2)}) copy-start(f32[1,128]{1,0:T(1,128)} %refs_5_.1) | copy-start | bytes 1540
  0.7 5.4 %collective-permute-start.1 = (f32[6,1,128]{2,1,0:T(1,128)}, f32[6,1,128]{2,1,0:T(1,128)S(1)}, u32[]{:S(2)}, u32[]{:S(2)}) collective-permute-start(f32[6,1,128]{2,1,0:T(1,128)} %bitcast.3), channel_id=1, source_target_pairs={{1,2},{3,4},{5,6},{2,1},{4,3},{6,5},{9,10},{11,12},{13,14},{10,9},... | collective-permute-start | bytes 9224 | tf_op jit(solution)/shard_map/ppermute | solution.py:203
  1.5 5.6 %collective-permute-start = (f32[6,1,128]{2,1,0:T(1,128)}, f32[6,1,128]{2,1,0:T(1,128)S(1)}, u32[]{:S(2)}, u32[]{:S(2)}) collective-permute-start(f32[6,1,128]{2,1,0:T(1,128)} %bitcast.4), channel_id=1, source_target_pairs={{0,1},{2,3},{4,5},{6,7},{1,0},{3,2},{5,4},{7,6},{8,9},{10,11},{12,... | collective-permute-start | bytes 9224 | tf_op jit(solution)/shard_map/ppermute | solution.py:202
  7.2 17.3 %copy-start = (bf16[1,128,1024]{2,1,0:T(8,128)(2,1)S(1)}, bf16[1,128,1024]{2,1,0:T(8,128)(2,1)}, u32[]{:S(2)}) copy-start(bf16[1,128,1024]{2,1,0:T(8,128)(2,1)} %inverse_ref.1) | copy-start | bytes 786436
  12.2 4.1 %collective-permute-start.2 = (bf16[1,128]{1,0:T(2,128)(2,1)S(1)}, bf16[1,128]{1,0:T(2,128)(2,1)S(1)}, u32[]{:S(2)}, u32[]{:S(2)}) collective-permute-start(bf16[1,128]{1,0:T(2,128)(2,1)S(1)} %get-tuple-element.5), channel_id=1, source_target_pairs={{0,1},{2,3},{4,5},{6,7},{1,0},{3,2},{5,4},{7,6},{8,9},{10,11},{12,... | collective-permute-start | bytes 776 | tf_op jit(solution)/shard_map/ppermute | solution.py:243
  16.3 5.4 %collective-permute-start.5 = (bf16[2,128]{1,0:T(2,128)(2,1)S(1)}, bf16[2,128]{1,0:T(2,128)(2,1)S(1)}, u32[]{:S(2)}, u32[]{:S(2)}) collective-permute-start(bf16[2,128]{1,0:T(2,128)(2,1)S(1)} %pad_maximum_fusion.refs_0_), channel_id=1, source_target_pairs={{0,6},{1,7},{2,4},{3,5},{4,2},{5,3},{6,0},{7,1},{8,14},{9,15},{10,... | collective-permute-start | bytes 1544 | tf_op jit(solution)/shard_map/ppermute | solution.py:246
  20.1 4.4 %collective-permute-start.4 = (bf16[2,128]{1,0:T(2,128)(2,1)S(1)}, bf16[2,128]{1,0:T(2,128)(2,1)S(1)}, u32[]{:S(2)}, u32[]{:S(2)}) collective-permute-start(bf16[2,128]{1,0:T(2,128)(2,1)S(1)} %pad_maximum_fusion.refs_0_), channel_id=1, source_target_pairs={{0,4},{1,5},{2,6},{3,7},{4,0},{5,1},{6,2},{7,3},{8,12},{9,13},{10,... | collective-permute-start | bytes 1544 | tf_op jit(solution)/shard_map/ppermute | solution.py:246
  20.1 4.4 %collective-permute-start.3 = (bf16[2,128]{1,0:T(2,128)(2,1)S(1)}, bf16[2,128]{1,0:T(2,128)(2,1)S(1)}, u32[]{:S(2)}, u32[]{:S(2)}) collective-permute-start(bf16[2,128]{1,0:T(2,128)(2,1)S(1)} %pad_maximum_fusion.refs_0_), channel_id=1, source_target_pairs={{0,2},{1,3},{2,0},{3,1},{4,6},{5,7},{6,4},{7,5},{8,10},{9,11},{10,... | collective-permute-start | bytes 1544 | tf_op jit(solution)/shard_map/ppermute | solution.py:246

commit v2 on v1

v2 whole, which is shorter than its diff:
```python
import functools

import jax
import jax.numpy as jnp
from jax import lax
from jax.experimental import pallas as pl
from jax.experimental.pallas import tpu as pltpu
from jax.sharding import PartitionSpec as P

BATCH = 128
GROUP = 8
TILE = 32
EDGE = 2
NEAR_CHIPS = 4
MIB = 1 << 20
F32 = jnp.float32
BF16 = jnp.bfloat16
NT = (((1,), (1,)), ((), ()))


def dot(a, b):
    return jnp.dot(a, b, preferred_element_type=F32)


def dot_nt(a, b, precision=None):
    return lax.dot_general(a, b, NT, precision=precision, preferred_element_type=F32)


def halves(x):
    high = x.astype(BF16)
    return high, (x - high.astype(F32)).astype(BF16)


def silu(a):
    half = 0.5 * a
    return half + half * jnp.tanh(half)


def list_alive(route_ref, list_ref, batches):
    count = jnp.int32(0)
    for b in range(batches):
        list_ref[count] = jnp.int32(b)
        count = count + (route_ref[0, 0, b] >= 0).astype(jnp.int32)
    return count


def stack_rows(ref):
    return jnp.concatenate([ref[k] for k in range(ref.shape[0])], axis=0)


def strain_of(own, before, after, neighbours_ref):
    points = own.shape[1]
    place = lax.broadcasted_iota(jnp.int32, own.shape, 1)
    left = jnp.where(place == 0, before, pltpu.roll(own, 1, 1))
    right = jnp.where(place == points - 1, after, pltpu.roll(own, points - 1, 1))
    first, second = neighbours_ref[0:1, :], neighbours_ref[1:2, :]
    lower = jnp.where(first == place, left, own)
    upper = jnp.where(second == place + 2, right, own)
    return (upper - lower) / (second - first).astype(F32)


def elastic_kernel(
    per_point,
    pick_ref,
    field_ref,
    neighbours_ref,
    loads_ref,
    stiffness_ref,
    state_ref,
    elastic_ref,
    sum_ref,
    point_ref,
):
    own = stack_rows(field_ref)
    points = own.shape[1]
    modes = state_ref.shape[2]
    tile = TILE * per_point
    strain = strain_of(own, jnp.zeros_like(own), jnp.zeros_like(own), neighbours_ref)
    load = lax.dot_general(
        strain,
        stack_rows(loads_ref),
        (((0,), (0,)), ((), ())),
        precision=lax.Precision.HIGHEST,
        preferred_element_type=F32,
    )
    stiffness = stiffness_ref[0]
    shift = dot(jnp.concatenate(halves(load), axis=0), stiffness)
    point_ref[...] = shift[:points, :] + shift[points:, :]
    for t in range(points // TILE):
        span, at = slice(t * tile, (t + 1) * tile), slice(t * TILE, (t + 1) * TILE)
        acc = dot(state_ref[0, span, :], stiffness)
        acc = acc.reshape(TILE, per_point, modes) + point_ref[at, :][:, None, :]
        elastic_ref[span, :] = acc.reshape(tile, modes).astype(BF16)
        sum_ref[at, :] = dot(pick_ref[...], elastic_ref[span, :])


def plastic_kernel(
    per_point,
    width,
    route_ref,
    core_ref,
    chip_ref,
    field_ref,
    neighbours_ref,
    loads_ref,
    stiffness_ref,
    state_ref,
    expand_ref,
    contract_ref,
    flags_ref,
    readout_ref,
    force_ref,
    elastic_ref,
    start_ref,
    out_ref,
    residual_ref,
    list_ref,
    sum_ref,
    edge_ref,
    taken_ref,
    hidden_ref,
    next_ref,
    bulk_sem,
    edge_sems,
    batch_sem,
):
    rows, modes = elastic_ref.shape
    points = rows // per_point
    batches = rows // BATCH
    edge = EDGE * per_point
    middle = slice(edge, rows - edge)
    bulk = pltpu.make_async_copy(elastic_ref.at[middle, :], out_ref.at[0, middle, :], bulk_sem)
    bulk.start()

    odd = lax.axis_index("sub") % 2 == 1
    own, core, chip = stack_rows(field_ref), stack_rows(core_ref), stack_rows(chip_ref)
    before = pltpu.roll(jnp.where(odd, core, chip), 1, 1)
    after = pltpu.roll(jnp.where(odd, chip, core), points - 1, 1)
    strain = strain_of(own, before, after, neighbours_ref)
    loads = stack_rows(loads_ref)
    near = [p % points for p in range(-EDGE, EDGE)]
    near = near[EDGE:] + near[:EDGE]
    load = jnp.concatenate(
        [jnp.sum(strain[:, p : p + 1] * loads, axis=0, keepdims=True) for p in near], axis=0
    )
    high, low = halves(load)
    blank = jnp.zeros((GROUP, modes), F32)
    extra = jnp.concatenate([high.astype(F32), low.astype(F32), blank], axis=0).astype(BF16)
    ends = [slice(0, edge), slice(rows - edge, rows)]
    acc = dot(
        jnp.concatenate([state_ref[0, s, :] for s in ends] + [extra], axis=0), stiffness_ref[0]
    )
    shift = acc[2 * edge : 2 * edge + 2 * EDGE, :] + acc[2 * edge + 2 * EDGE : 2 * edge + 4 * EDGE, :]
    fixed = acc[: 2 * edge, :].reshape(2 * EDGE, per_point, modes) + shift[:, None, :]
    fixed = fixed.reshape(2 * edge, modes).astype(BF16)
    edge_ref[...] = fixed
    totals = jnp.sum(fixed.astype(F32).reshape(2 * EDGE, per_point, modes), axis=1)
    sum_ref[...] = start_ref[...]
    sum_ref[0:EDGE, :] = totals[:EDGE, :]
    sum_ref[points - EDGE : points, :] = totals[EDGE:, :]
    edges = [
        pltpu.make_async_copy(edge_ref.at[i * edge : (i + 1) * edge, :], out_ref.at[0, s, :], edge_sems.at[i])
        for i, s in enumerate(ends)
    ]
    for copy in edges:
        copy.start()

    count = list_alive(route_ref, list_ref, batches)

    @pl.loop(0, (count + width - 1) // width)
    def _(c):
        chosen = [list_ref[jnp.minimum(c * width + j, count - 1)] for j in range(width)]
        starts = [pl.multiple_of(b * BATCH, BATCH) for b in chosen]
        for j, (b, s) in enumerate(zip(chosen, starts)):
            taken_ref[j * BATCH : (j + 1) * BATCH, :] = elastic_ref[pl.ds(s, BATCH), :]

            @pl.when(b == 0)
            def _():
                taken_ref[j * BATCH : j * BATCH + edge, :] = edge_ref[:edge, :]

            @pl.when(b == batches - 1)
            def _():
                taken_ref[(j + 1) * BATCH - edge : (j + 1) * BATCH, :] = edge_ref[edge:, :]

        taken = taken_ref[...]
        for h in range(0, expand_ref.shape[2], 512):
            hidden_ref[:, h : h + 512] = silu(dot(taken, expand_ref[0, :, h : h + 512])).astype(BF16)
        correction = dot(hidden_ref[...], contract_ref[0])
        p = lax.broadcasted_iota(jnp.int32, (points, BATCH), 0) * per_point
        r = lax.broadcasted_iota(jnp.int32, (points, BATCH), 1)
        owners, changes = [], []
        for j, s in enumerate(starts):
            at = slice(j * BATCH, (j + 1) * BATCH)
            flags = flags_ref[0:1, pl.ds(s, BATCH)].astype(F32)
            column = jnp.broadcast_to(flags, (BATCH, BATCH)).T
            column = jnp.concatenate([column] * (modes // BATCH), axis=1)
            change = column * correction[at, :]
            slot = pl.multiple_of((c * width + j) * BATCH, BATCH)
            next_ref[pl.ds(slot, BATCH), :] = (taken[at, :].astype(F32) + change).astype(BF16)
            row = r + jnp.where(c * width + j < count, s, -rows)
            owners.append(jnp.where((row >= p) & (row < p + per_point), 1.0, 0.0).astype(BF16))
            changes.append(change.astype(BF16))
        sum_ref[...] += dot(jnp.concatenate(owners, axis=1), jnp.concatenate(changes, axis=0))

    for copy in [bulk] + edges:
        copy.wait()

    def changed(i):
        source = pl.ds(pl.multiple_of(i * BATCH, BATCH), BATCH)
        target = pl.ds(pl.multiple_of(list_ref[i] * BATCH, BATCH), BATCH)
        return pltpu.make_async_copy(next_ref.at[source, :], out_ref.at[0, target, :], batch_sem)

    @pl.loop(0, count)
    def _(i):
        changed(i).start()

    readout = jnp.broadcast_to(readout_ref[...], (GROUP, modes)).astype(F32)
    mean = dot_nt(readout, sum_ref[...], lax.Precision.HIGHEST)[0:1, :] * (1.0 / per_point)
    residual_ref[...] = (force_ref[...] - mean).astype(BF16)

    @pl.loop(0, count)
    def _(i):
        changed(i).wait()


def pick_kernel(per_point, pick_ref):
    shape = pick_ref.shape
    p = lax.broadcasted_iota(jnp.int32, shape, 0)
    r = lax.broadcasted_iota(jnp.int32, shape, 1)
    pick_ref[...] = jnp.where((r >= p * per_point) & (r < (p + 1) * per_point), 1.0, 0.0).astype(BF16)


def coarse_kernel(inverse_ref, *refs):
    pairs, out_ref = refs[:-1], refs[-1]
    points = out_ref.shape[1]
    me = lax.axis_index("sub")
    total = jnp.zeros((GROUP, points), F32)
    for k, pair_ref in enumerate(pairs):
        chip = (me // 2) ^ k
        for c in range(2):
            block = pl.multiple_of((2 * chip + (me + c) % 2) * points, points)
            part = jnp.broadcast_to(pair_ref[c : c + 1, :], (GROUP, points))
            total = total + dot_nt(part, inverse_ref[0, :, pl.ds(block, points)])
    out_ref[...] = total[0:1, :]


def swap_pairs(n, offset):
    pairs = [(i, i + 1) for i in range(offset, n - 1, 2)]
    return pairs + [(j, i) for i, j in pairs]


def on_device(
    displacement,
    neighbours,
    micro_state,
    strain_loads,
    stiffness,
    expand_weight,
    contract_weight,
    batch_route,
    yield_flags,
    readout,
    external_force,
    coarse_inverse,
):
    n = lax.axis_size("sub")
    points = displacement.shape[2]
    rows, modes = micro_state.shape[1:]
    hidden_size = expand_weight.shape[2]
    per_point = rows // points
    batches = rows // BATCH
    reach = min(16, n // 2, batches)
    width = min(4, reach)
    slots = -(-reach // width) * width
    field = jnp.transpose(displacement, (1, 0, 2))
    loads = jnp.transpose(strain_loads, (1, 0, 2))
    vmem = pl.BlockSpec(memory_space=pltpu.VMEM)
    pick = pl.pallas_call(
        functools.partial(pick_kernel, per_point),
        out_shape=jax.ShapeDtypeStruct((TILE, TILE * per_point), BF16),
        out_specs=vmem,
        compiler_params=pltpu.CompilerParams(vmem_limit_bytes=MIB),
        cost_estimate=pl.CostEstimate(flops=20 * 10**9, bytes_accessed=MIB, transcendentals=0),
    )()
    from_core = lax.ppermute(field, "sub", swap_pairs(n, 0))
    from_chip = lax.ppermute(field, "sub", swap_pairs(n, 1))
    elastic, sums = pl.pallas_call(
        functools.partial(elastic_kernel, per_point),
        out_shape=(
            jax.ShapeDtypeStruct((rows, modes), BF16),
            jax.ShapeDtypeStruct((points, modes), F32),
        ),
        in_specs=[vmem] * 6,
        out_specs=(vmem, vmem),
        scratch_shapes=[pltpu.VMEM((points, modes), F32)],
        compiler_params=pltpu.CompilerParams(vmem_limit_bytes=20 * MIB),
        cost_estimate=pl.CostEstimate(
            flops=2 * rows * modes * modes, bytes_accessed=8 * MIB, transcendentals=0
        ),
    )(pick, field, neighbours, loads, stiffness, micro_state)
    states_next, residual = pl.pallas_call(
        functools.partial(plastic_kernel, per_point, width),
        out_shape=(
            jax.ShapeDtypeStruct((1, rows, modes), BF16),
            jax.ShapeDtypeStruct((1, points), BF16),
        ),
        in_specs=[pl.BlockSpec(memory_space=pltpu.SMEM)] + [vmem] * 14,
        out_specs=(pl.BlockSpec(memory_space=pltpu.HBM), vmem),
        scratch_shapes=[
            pltpu.SMEM((batches + 1,), jnp.int32),
            pltpu.VMEM((points, modes), F32),
            pltpu.VMEM((2 * EDGE * per_point, modes), BF16),
            pltpu.VMEM((width * BATCH, modes), BF16),
            pltpu.VMEM((width * BATCH, hidden_size), BF16),
            pltpu.VMEM((slots * BATCH, modes), BF16),
            pltpu.SemaphoreType.DMA(()),
            pltpu.SemaphoreType.DMA((2,)),
            pltpu.SemaphoreType.DMA(()),
        ],
        compiler_params=pltpu.CompilerParams(vmem_limit_bytes=28 * MIB),
        cost_estimate=pl.CostEstimate(
            flops=4 * width * BATCH * modes * hidden_size, bytes_accessed=8 * MIB, transcendentals=0
        ),
    )(
        batch_route,
        from_core,
        from_chip,
        field,
        neighbours,
        loads,
        stiffness,
        micro_state,
        expand_weight,
        contract_weight,
        yield_flags,
        readout,
        external_force,
        elastic,
        sums,
    )
    if n // 2 > NEAR_CHIPS:
        everyone = lax.all_gather(residual, "sub", axis=1, tiled=True)[0]
        return states_next, dot(coarse_inverse[0], everyone)[None]
    other = lax.ppermute(residual, "sub", swap_pairs(n, 0))
    pair = jnp.concatenate([residual, other], axis=0)
    pairs = [pair] + [
        lax.ppermute(pair, "sub", [(i, i ^ (2 * k)) for i in range(n)]) for k in range(1, n // 2)
    ]
    coarse = pl.pallas_call(
        coarse_kernel,
        out_shape=jax.ShapeDtypeStruct((1, points), F32),
        in_specs=[vmem] * (1 + len(pairs)),
        out_specs=vmem,
        compiler_params=pltpu.CompilerParams(vmem_limit_bytes=4 * MIB),
    )(coarse_inverse, *pairs)
    return (states_next, coarse)


def solution(mesh):
    return jax.shard_map(
        on_device,
        mesh=mesh,
        in_specs=(
            P("variant", None, "sub"),
            P(None, "sub"),
            P("variant", "sub", None),
            P("variant", None, None),
            P("variant", None, None),
            P("variant", None, None),
            P("variant", None, None),
            P("variant", None, "sub"),
            P("variant", "sub"),
            P("variant", None),
            P("variant", "sub"),
            P("variant", "sub", None),
        ),
        out_specs=(P("variant", "sub", None), P("variant", "sub")),
        check_vma=False,
    )
```

time: 25.5 us -> 22.7 us (0.89)
  starting transfers between devices: 13.1 us -> 10.6 us
  waiting for transfers between devices: 5.62 us -> 4.64 us
  Pallas kernels: 5.72 us -> 6.47 us
    ppermute x1, starting transfers between devices: 3.26 us -> 0.09 us  [on_device(): other = lax.ppermute(residual, 'sub', swap_pairs(n, 0))]
    ppermute x1, waiting for transfers between devices: 1 us -> 0.01 us  [on_device(): from_core = lax.ppermute(field, 'sub', swap_pairs(n, 0))]
    pallas_call x1 -> x2, Pallas kernels: 4.92 us -> 5.68 us  [the longest x1 3.06 us: on_device(): pl.pallas_call(functools.partial(elastic_kernel, per_point), out_shape=(j...]
    ppermute x3, starting transfers between devices: 4.5 us -> 5.13 us  [on_device(): lax.ppermute(pair, 'sub', [(i, i ^ 2 * k) for i in range(n)])]
    ppermute x1, waiting for transfers between devices: 0.82 us -> 1.09 us  [on_device(): other = lax.ppermute(residual, 'sub', swap_pairs(n, 0))]
    ppermute x3, waiting for transfers between devices: 3.8 us -> 3.54 us  [on_device(): lax.ppermute(pair, 'sub', [(i, i ^ 2 * k) for i in range(n)])]
  transfers between devices with their start and end apart: 6 -> 6, of which waited for: 4 -> 4; matrix products, arithmetic and copies ran while one was open for 0% -> 0% of each run, Pallas kernels for 0% -> 14%
where the time goes in v2:
time: 22.7 us; the launch traced here: 22.6 us
  starting transfers between devices  10.6 us (47%)
  Pallas kernels  6.47 us (29%)
  waiting for transfers between devices  4.64 us (20%)
  between operations  0.85 us (4%)
    ppermute x3, starting transfers between devices, on_device(): lax.ppermute(pair, 'sub', [(i, i ^ 2 * k) for i in range(n)])  5.13 us
    ppermute x1, starting transfers between devices, on_device(): from_core = lax.ppermute(field, 'sub', swap_pairs(n, 0))  4.58 us
    ppermute x3, waiting for transfers between devices, on_device(): lax.ppermute(pair, 'sub', [(i, i ^ 2 * k) for i in range(n)])  3.54 us
    pallas_call x1, Pallas kernels, on_device(): pl.pallas_call(functools.partial(elastic_kernel, per_point), out_shape=(j...  3.06 us
    pallas_call x1, Pallas kernels, on_device(): pl.pallas_call(functools.partial(plastic_kernel, per_point, width), out_s...  2.62 us
    ppermute x1, waiting for transfers between devices, on_device(): other = lax.ppermute(residual, 'sub', swap_pairs(n, 0))  1.09 us
    ppermute x1, starting transfers between devices, on_device(): from_chip = lax.ppermute(field, 'sub', swap_pairs(n, 1))  0.79 us
    pallas_call x1, Pallas kernels, on_device(): pl.pallas_call(coarse_kernel, out_shape=jax.ShapeDtypeStruct((1, points),...  0.77 us
  transfers between devices with their start and end apart: 6, of which 4 were waited for; matrix products, arithmetic and copies ran while one was open for 0% of the time, Pallas kernels for 14%

profile of v2, /device:TPU:0, one launch (start us, length us, event | category | flops | bytes accessed | tf_op | source)
XLA Modules:
  0.0 22.6 jit_solution(12421977568927856604)
XLA Ops:
  0.6 0.0 copy-start
  0.6 0.0 copy-start.3
  0.7 0.0 copy-start.5
  0.7 0.0 copy-start.7
  0.7 0.0 copy-start.10
  0.7 0.8 %collective-permute-start.1 = (f32[6,1,128]{2,1,0:T(1,128)}, f32[6,1,128]{2,1,0:T(1,128)S(1)}, u32[]{:S(2)}, u32[]{:S(2)}) collective-permute-start(f32[6,1,128]{2,1,0:T(1,128)} %bitcast.4), channel_id=1, source_target_pairs={{1,2},{3,4},{5,6},{2,1},{4,3},{6,5},{9,10},{11,12},{13,14},{10,9},... | collective-permute-start | bytes 9224 | tf_op jit(solution)/shard_map/ppermute | solution.py:286
  1.5 4.6 %collective-permute-start = (f32[6,1,128]{2,1,0:T(1,128)}, f32[6,1,128]{2,1,0:T(1,128)S(1)}, u32[]{:S(2)}, u32[]{:S(2)}) collective-permute-start(f32[6,1,128]{2,1,0:T(1,128)} %bitcast.5), channel_id=1, source_target_pairs={{0,1},{2,3},{4,5},{6,7},{1,0},{3,2},{5,4},{7,6},{8,9},{10,11},{12,... | collective-permute-start | bytes 9224 | tf_op jit(solution)/shard_map/ppermute | solution.py:285
  6.1 0.0 copy-start.1
  6.1 0.0 copy-start.2
  6.1 0.0 copy-start.6
  6.1 0.0 copy-start.8
  6.1 0.0 copy-start.9
  6.1 0.0 copy-start.11
  6.2 0.0 copy-done
  6.2 0.0 copy-done.3
  6.2 0.0 copy-done.5
  6.2 0.0 copy-done.7
  6.2 0.0 copy-done.10
  6.2 3.1 %shard_map.132 = (bf16[3072,512]{1,0:T(8,128)(2,1)S(1)}, f32[128,512]{1,0:T(8,128)S(1)}) custom-call(bf16[32,768]{1,0:T(8,128)(2,1)S(1)} %shard_map.131.pick_ref, f32[6,1,128]{2,1,0:T(1,128)S(1)} %bitcast.6, s32[2,128]{1,0:T(2,128)S(1)} %copy-done.10, f32[6,1,512]{2,1,0:T(1,128)S(1)} %bitcast.2, bf16[1,512,512]{2,1,0:T(8,128)(2,1)S(1)} %copy-done.3, ...), custom_call_target="tpu_custom_call" | custom-call | flops 1610612736 | bytes 8388608 | tf_op jit(solution)/shard_map/pallas_call | solution.py:287
  9.3 0.0 collective-permute-done.1.chip_ref
  9.3 0.0 collective-permute-done.core_ref
  9.3 0.0 copy-done.1
  9.3 0.0 copy-done.2
  9.3 0.0 copy-done.6
  9.3 0.0 copy-done.8
  9.3 0.0 copy-done.9
  9.3 0.0 copy-done.11
  9.3 0.0 copy-start.4
  9.4 2.6 %shard_map.133 = (bf16[1,3072,512]{2,1,0:T(8,128)(2,1)}, bf16[1,128]{1,0:T(2,128)(2,1)S(1)}) custom-call(s32[1,2,24]{2,1,0:T(2,128)S(1)} %copy-done.9, f32[6,1,128]{2,1,0:T(1,128)S(1)} %collective-permute-done.core_ref, f32[6,1,128]{2,1,0:T(1,128)S(1)} %collective-permute-done.1.chip_ref, f32[6,1,128]{2,1,0:T(1,128)S(1)} %bitcast.7, ...), custom_call_target="tpu_custom_call" | custom-call | flops 2147483648 | bytes 8388608 | tf_op jit(solution)/shard_map/pallas_call | solution.py:301
  12.0 0.1 collective-permute-start.2
  12.1 1.1 %collective-permute-done.2 = bf16[1,128]{1,0:T(2,128)(2,1)S(1)} collective-permute-done((bf16[1,128]{1,0:T(2,128)(2,1)S(1)}, bf16[1,128]{1,0:T(2,128)(2,1)S(1)}, u32[]{:S(2)}, u32[]{:S(2)}) %collective-permute-start.2) | collective-permute-done | bytes 288 | tf_op jit(solution)/shard_map/ppermute | solution.py:344
  13.2 4.1 %collective-permute-start.5 = (bf16[2,128]{1,0:T(2,128)(2,1)S(1)}, bf16[2,128]{1,0:T(2,128)(2,1)S(1)}, u32[]{:S(2)}, u32[]{:S(2)}) collective-permute-start(bf16[2,128]{1,0:T(2,128)(2,1)S(1)} %pad_maximum_fusion.refs_0_), channel_id=1, source_target_pairs={{0,6},{1,7},{2,4},{3,5},{4,2},{5,3},{6,0},{7,1},{8,14},{9,15},{10,... | collective-permute-start | bytes 1544 | tf_op jit(solution)/shard_map/ppermute | solution.py:347
  17.3 1.0 %collective-permute-start.4 = (bf16[2,128]{1,0:T(2,128)(2,1)S(1)}, bf16[2,128]{1,0:T(2,128)(2,1)S(1)}, u32[]{:S(2)}, u32[]{:S(2)}) collective-permute-start(bf16[2,128]{1,0:T(2,128)(2,1)S(1)} %pad_maximum_fusion.refs_0_), channel_id=1, source_target_pairs={{0,4},{1,5},{2,6},{3,7},{4,0},{5,1},{6,2},{7,3},{8,12},{9,13},{10,... | collective-permute-start | bytes 1544 | tf_op jit(solution)/shard_map/ppermute | solution.py:347
  18.3 0.0 collective-permute-start.3
  18.3 0.5 %collective-permute-done.5.refs_3_ = bf16[2,128]{1,0:T(2,128)(2,1)S(1)} collective-permute-done((bf16[2,128]{1,0:T(2,128)(2,1)S(1)}, bf16[2,128]{1,0:T(2,128)(2,1)S(1)}, u32[]{:S(2)}, u32[]{:S(2)}) %collective-permute-start.5) | collective-permute-done | bytes 544 | tf_op jit(solution)/shard_map/ppermute | solution.py:347
  18.8 2.9 %collective-permute-done.4.refs_2_ = bf16[2,128]{1,0:T(2,128)(2,1)S(1)} collective-permute-done((bf16[2,128]{1,0:T(2,128)(2,1)S(1)}, bf16[2,128]{1,0:T(2,128)(2,1)S(1)}, u32[]{:S(2)}, u32[]{:S(2)}) %collective-permute-start.4) | collective-permute-done | bytes 544 | tf_op jit(solution)/shard_map/ppermute | solution.py:347
  21.7 0.1 collective-permute-done.3.refs_1_
  21.9 0.0 copy-done.4
  21.9 0.8 %shard_map.134 = f32[1,128]{1,0:T(1,128)} custom-call(bf16[1,128,1024]{2,1,0:T(8,128)(2,1)S(1)} %copy-done.4, bf16[2,128]{1,0:T(2,128)(2,1)S(1)} %pad_maximum_fusion.refs_0_, bf16[2,128]{1,0:T(2,128)(2,1)S(1)} %collective-permute-done.3.refs_1_, bf16[2,128]{1,0:T(2,128)(2,1)S(1)} %collective-permute-done.4.refs_2_, ...), custom_call_target="tpu_custom_call" | custom-call | tf_op jit(solution)/shard_map/pallas_call | solution.py:349
  (2 shorter events, 0.0 us)
Async XLA Ops:
  0.6 5.5 %copy-start = (bf16[1,3072,512]{2,1,0:T(8,128)(2,1)S(1)}, bf16[1,3072,512]{2,1,0:T(8,128)(2,1)}, u32[]{:S(2)}) copy-start(bf16[1,3072,512]{2,1,0:T(8,128)(2,1)} %state_ref.3) | copy-start | bytes 9437188
  0.6 5.5 %copy-start.3 = (bf16[1,512,512]{2,1,0:T(8,128)(2,1)S(1)}, bf16[1,512,512]{2,1,0:T(8,128)(2,1)}, u32[]{:S(2)}) copy-start(bf16[1,512,512]{2,1,0:T(8,128)(2,1)} %stiffness_ref.3) | copy-start | bytes 1572868
  0.7 5.5 %copy-start.5 = (f32[1,6,512]{2,0,1:T(1,128)S(1)}, f32[1,6,512]{2,0,1:T(1,128)}, u32[]{:S(2)}) copy-start(f32[1,6,512]{2,0,1:T(1,128)} %param.15) | copy-start | bytes 36868
  0.7 5.5 %copy-start.7 = (f32[1,6,128]{2,0,1:T(1,128)S(1)}, f32[1,6,128]{2,0,1:T(1,128)}, u32[]{:S(2)}) copy-start(f32[1,6,128]{2,0,1:T(1,128)} %param.12) | copy-start | bytes 9220
  0.7 5.5 %copy-start.10 = (s32[2,128]{1,0:T(2,128)S(1)}, s32[2,128]{1,0:T(2,128)}, u32[]{:S(2)}) copy-start(s32[2,128]{1,0:T(2,128)} %neighbours_ref.3) | copy-start | bytes 3076
  0.7 8.6 %collective-permute-start.1 = (f32[6,1,128]{2,1,0:T(1,128)}, f32[6,1,128]{2,1,0:T(1,128)S(1)}, u32[]{:S(2)}, u32[]{:S(2)}) collective-permute-start(f32[6,1,128]{2,1,0:T(1,128)} %bitcast.4), channel_id=1, source_target_pairs={{1,2},{3,4},{5,6},{2,1},{4,3},{6,5},{9,10},{11,12},{13,14},{10,9},... | collective-permute-start | bytes 9224 | tf_op jit(solution)/shard_map/ppermute | solution.py:286
  1.5 7.8 %collective-permute-start = (f32[6,1,128]{2,1,0:T(1,128)}, f32[6,1,128]{2,1,0:T(1,128)S(1)}, u32[]{:S(2)}, u32[]{:S(2)}) collective-permute-start(f32[6,1,128]{2,1,0:T(1,128)} %bitcast.5), channel_id=1, source_target_pairs={{0,1},{2,3},{4,5},{6,7},{1,0},{3,2},{5,4},{7,6},{8,9},{10,11},{12,... | collective-permute-start | bytes 9224 | tf_op jit(solution)/shard_map/ppermute | solution.py:285
  6.1 3.2 %copy-start.1 = (bf16[1,512,2048]{2,1,0:T(8,128)(2,1)S(1)}, bf16[1,512,2048]{2,1,0:T(8,128)(2,1)}, u32[]{:S(2)}) copy-start(bf16[1,512,2048]{2,1,0:T(8,128)(2,1)} %expand_ref.1) | copy-start | bytes 6291460
  6.1 3.2 %copy-start.2 = (bf16[1,2048,512]{2,1,0:T(8,128)(2,1)S(1)}, bf16[1,2048,512]{2,1,0:T(8,128)(2,1)}, u32[]{:S(2)}) copy-start(bf16[1,2048,512]{2,1,0:T(8,128)(2,1)} %contract_ref.1) | copy-start | bytes 6291460
  6.1 3.2 %copy-start.6 = (s32[1,3072]{1,0:T(1,128)S(1)}, s32[1,3072]{1,0:T(1,128)}, u32[]{:S(2)}) copy-start(s32[1,3072]{1,0:T(1,128)} %flags_ref.1) | copy-start | bytes 36868
  6.1 3.2 %copy-start.8 = (bf16[1,512]{1,0:T(2,128)(2,1)S(1)}, bf16[1,512]{1,0:T(2,128)(2,1)}, u32[]{:S(2)}) copy-start(bf16[1,512]{1,0:T(2,128)(2,1)} %readout_ref.1) | copy-start | bytes 3076
  6.1 3.2 %copy-start.9 = (s32[1,2,24]{2,1,0:T(2,128)S(1)}, s32[1,2,24]{2,1,0:T(2,128)}, u32[]{:S(2)}) copy-start(s32[1,2,24]{2,1,0:T(2,128)} %route_ref.1) | copy-start | bytes 580
  6.1 3.2 %copy-start.11 = (f32[1,128]{1,0:T(1,128)S(1)}, f32[1,128]{1,0:T(1,128)}, u32[]{:S(2)}) copy-start(f32[1,128]{1,0:T(1,128)} %force_ref.1) | copy-start | bytes 1540
  9.3 12.5 %copy-start.4 = (bf16[1,128,1024]{2,1,0:T(8,128)(2,1)S(1)}, bf16[1,128,1024]{2,1,0:T(8,128)(2,1)}, u32[]{:S(2)}) copy-start(bf16[1,128,1024]{2,1,0:T(8,128)(2,1)} %inverse_ref.1) | copy-start | bytes 786436
  12.0 1.2 %collective-permute-start.2 = (bf16[1,128]{1,0:T(2,128)(2,1)S(1)}, bf16[1,128]{1,0:T(2,128)(2,1)S(1)}, u32[]{:S(2)}, u32[]{:S(2)}) collective-permute-start(bf16[1,128]{1,0:T(2,128)(2,1)S(1)} %get-tuple-element.9), channel_id=1, source_target_pairs={{0,1},{2,3},{4,5},{6,7},{1,0},{3,2},{5,4},{7,6},{8,9},{10,11},{12,... | collective-permute-start | bytes 776 | tf_op jit(solution)/shard_map/ppermute | solution.py:344
  13.2 5.6 %collective-permute-start.5 = (bf16[2,128]{1,0:T(2,128)(2,1)S(1)}, bf16[2,128]{1,0:T(2,128)(2,1)S(1)}, u32[]{:S(2)}, u32[]{:S(2)}) collective-permute-start(bf16[2,128]{1,0:T(2,128)(2,1)S(1)} %pad_maximum_fusion.refs_0_), channel_id=1, source_target_pairs={{0,6},{1,7},{2,4},{3,5},{4,2},{5,3},{6,0},{7,1},{8,14},{9,15},{10,... | collective-permute-start | bytes 1544 | tf_op jit(solution)/shard_map/ppermute | solution.py:347
  17.3 4.4 %collective-permute-start.4 = (bf16[2,128]{1,0:T(2,128)(2,1)S(1)}, bf16[2,128]{1,0:T(2,128)(2,1)S(1)}, u32[]{:S(2)}, u32[]{:S(2)}) collective-permute-start(bf16[2,128]{1,0:T(2,128)(2,1)S(1)} %pad_maximum_fusion.refs_0_), channel_id=1, source_target_pairs={{0,4},{1,5},{2,6},{3,7},{4,0},{5,1},{6,2},{7,3},{8,12},{9,13},{10,... | collective-permute-start | bytes 1544 | tf_op jit(solution)/shard_map/ppermute | solution.py:347
  18.3 3.5 %collective-permute-start.3 = (bf16[2,128]{1,0:T(2,128)(2,1)S(1)}, bf16[2,128]{1,0:T(2,128)(2,1)S(1)}, u32[]{:S(2)}, u32[]{:S(2)}) collective-permute-start(bf16[2,128]{1,0:T(2,128)(2,1)S(1)} %pad_maximum_fusion.refs_0_), channel_id=1, source_target_pairs={{0,2},{1,3},{2,0},{3,1},{4,6},{5,7},{6,4},{7,5},{8,10},{9,11},{10,... | collective-permute-start | bytes 1544 | tf_op jit(solution)/shard_map/ppermute | solution.py:347

commit v3 on v2

--- a/solution.py
+++ b/solution.py
@@ -46,6 +46,24 @@
 
 def stack_rows(ref):
     return jnp.concatenate([ref[k] for k in range(ref.shape[0])], axis=0)
+
+
+def thirds(x):
+    high = x.astype(BF16).astype(F32)
+    middle = (x - high).astype(BF16).astype(F32)
+    return high, middle, x - high - middle
+
+
+def spread(strain, loads):
+    blank = [jnp.zeros((GROUP - strain.shape[0] % GROUP, x.shape[1]), F32) for x in (strain, loads)]
+    a, b, c = (jnp.concatenate([x, blank[0]], axis=0) for x in thirds(strain))
+    d, e, f = (jnp.concatenate([x, blank[1]], axis=0) for x in thirds(loads))
+    return lax.dot_general(
+        jnp.concatenate([a, a, b, b, a, c], axis=0).astype(BF16),
+        jnp.concatenate([d, e, d, e, f, d], axis=0).astype(BF16),
+        (((0,), (0,)), ((), ())),
+        preferred_element_type=F32,
+    )
 
 
 def strain_of(own, before, after, neighbours_ref):
@@ -76,13 +94,7 @@
     modes = state_ref.shape[2]
     tile = TILE * per_point
     strain = strain_of(own, jnp.zeros_like(own), jnp.zeros_like(own), neighbours_ref)
-    load = lax.dot_general(
-        strain,
-        stack_rows(loads_ref),
-        (((0,), (0,)), ((), ())),
-        precision=lax.Precision.HIGHEST,
-        preferred_element_type=F32,
-    )
+    load = spread(strain, stack_rows(loads_ref))
     stiffness = stiffness_ref[0]
     shift = dot(jnp.concatenate(halves(load), axis=0), stiffness)
     point_ref[...] = shift[:points, :] + shift[points:, :]
@@ -114,15 +126,13 @@
     start_ref,
     out_ref,
     residual_ref,
+    next_ref,
     list_ref,
     sum_ref,
     edge_ref,
-    taken_ref,
     hidden_ref,
-    next_ref,
     bulk_sem,
     edge_sems,
-    batch_sem,
 ):
     rows, modes = elastic_ref.shape
     points = rows // per_point
@@ -131,6 +141,7 @@
     middle = slice(edge, rows - edge)
     bulk = pltpu.make_async_copy(elastic_ref.at[middle, :], out_ref.at[0, middle, :], bulk_sem)
     bulk.start()
+    count = list_alive(route_ref, list_ref, batches)
 
     odd = lax.axis_index("sub") % 2 == 1
     own, core, chip = stack_rows(field_ref), stack_rows(core_ref), stack_rows(chip_ref)
@@ -165,24 +176,16 @@
     for copy in edges:
         copy.start()
 
-    count = list_alive(route_ref, list_ref, batches)
-
-    @pl.loop(0, (count + width - 1) // width)
-    def _(c):
-        chosen = [list_ref[jnp.minimum(c * width + j, count - 1)] for j in range(width)]
+    def chunk(c):
+        chosen = [list_ref[jnp.maximum(jnp.minimum(c * width + j, count - 1), 0)] for j in range(width)]
         starts = [pl.multiple_of(b * BATCH, BATCH) for b in chosen]
-        for j, (b, s) in enumerate(zip(chosen, starts)):
-            taken_ref[j * BATCH : (j + 1) * BATCH, :] = elastic_ref[pl.ds(s, BATCH), :]
-
-            @pl.when(b == 0)
-            def _():
-                taken_ref[j * BATCH : j * BATCH + edge, :] = edge_ref[:edge, :]
-
-            @pl.when(b == batches - 1)
-            def _():
-                taken_ref[(j + 1) * BATCH - edge : (j + 1) * BATCH, :] = edge_ref[edge:, :]
-
-        taken = taken_ref[...]
+        parts = []
+        for b, s in zip(chosen, starts):
+            part = elastic_ref[pl.ds(s, BATCH), :]
+            parts.append(jnp.where(b == 0, fixed[:edge, :], part[:edge, :]))
+            parts.append(part[edge : BATCH - edge, :])
+            parts.append(jnp.where(b == batches - 1, fixed[edge:, :], part[BATCH - edge :, :]))
+        taken = jnp.concatenate(parts, axis=0)
         for h in range(0, expand_ref.shape[2], 512):
             hidden_ref[:, h : h + 512] = silu(dot(taken, expand_ref[0, :, h : h + 512])).astype(BF16)
         correction = dot(hidden_ref[...], contract_ref[0])
@@ -202,21 +205,28 @@
             changes.append(change.astype(BF16))
         sum_ref[...] += dot(jnp.concatenate(owners, axis=1), jnp.concatenate(changes, axis=0))
 
+    pl.loop(0, (count + width - 1) // width)(chunk)
+
+    readout = jnp.broadcast_to(readout_ref[...], (GROUP, modes))
+    parts = dot_nt(readout, jnp.concatenate(halves(sum_ref[...]), axis=0))[0:1, :]
+    mean = (parts[:, :points] + parts[:, points:]) * (1.0 / per_point)
+    residual_ref[...] = (force_ref[...] - mean).astype(BF16)
     for copy in [bulk] + edges:
         copy.wait()
+
+
+def write_kernel(route_ref, next_ref, states_ref, out_ref, list_ref, sem):
+    del states_ref
+    count = list_alive(route_ref, list_ref, route_ref.shape[2])
 
     def changed(i):
         source = pl.ds(pl.multiple_of(i * BATCH, BATCH), BATCH)
         target = pl.ds(pl.multiple_of(list_ref[i] * BATCH, BATCH), BATCH)
-        return pltpu.make_async_copy(next_ref.at[source, :], out_ref.at[0, target, :], batch_sem)
+        return pltpu.make_async_copy(next_ref.at[source, :], out_ref.at[0, target, :], sem)
 
     @pl.loop(0, count)
     def _(i):
         changed(i).start()
-
-    readout = jnp.broadcast_to(readout_ref[...], (GROUP, modes)).astype(F32)
-    mean = dot_nt(readout, sum_ref[...], lax.Precision.HIGHEST)[0:1, :] * (1.0 / per_point)
-    residual_ref[...] = (force_ref[...] - mean).astype(BF16)
 
     @pl.loop(0, count)
     def _(i):
@@ -234,13 +244,14 @@
     pairs, out_ref = refs[:-1], refs[-1]
     points = out_ref.shape[1]
     me = lax.axis_index("sub")
-    total = jnp.zeros((GROUP, points), F32)
+    values, columns = [], []
     for k, pair_ref in enumerate(pairs):
         chip = (me // 2) ^ k
         for c in range(2):
             block = pl.multiple_of((2 * chip + (me + c) % 2) * points, points)
-            part = jnp.broadcast_to(pair_ref[c : c + 1, :], (GROUP, points))
-            total = total + dot_nt(part, inverse_ref[0, :, pl.ds(block, points)])
+            values.append(jnp.broadcast_to(pair_ref[c : c + 1, :], (GROUP, points)))
+            columns.append(inverse_ref[0, :, pl.ds(block, points)])
+    total = dot_nt(jnp.concatenate(values, axis=1), jnp.concatenate(columns, axis=1))
     out_ref[...] = total[0:1, :]
 
 
@@ -275,6 +286,8 @@
     field = jnp.transpose(displacement, (1, 0, 2))
     loads = jnp.transpose(strain_loads, (1, 0, 2))
     vmem = pl.BlockSpec(memory_space=pltpu.VMEM)
+    smem = pl.BlockSpec(memory_space=pltpu.SMEM)
+    hbm = pl.BlockSpec(memory_space=pltpu.HBM)
     pick = pl.pallas_call(
         functools.partial(pick_kernel, per_point),
         out_shape=jax.ShapeDtypeStruct((TILE, TILE * per_point), BF16),
@@ -298,24 +311,22 @@
             flops=2 * rows * modes * modes, bytes_accessed=8 * MIB, transcendentals=0
         ),
     )(pick, field, neighbours, loads, stiffness, micro_state)
-    states_next, residual = pl.pallas_call(
+    states, residual, updated = pl.pallas_call(
         functools.partial(plastic_kernel, per_point, width),
         out_shape=(
             jax.ShapeDtypeStruct((1, rows, modes), BF16),
             jax.ShapeDtypeStruct((1, points), BF16),
+            jax.ShapeDtypeStruct((slots * BATCH, modes), BF16),
         ),
-        in_specs=[pl.BlockSpec(memory_space=pltpu.SMEM)] + [vmem] * 14,
-        out_specs=(pl.BlockSpec(memory_space=pltpu.HBM), vmem),
+        in_specs=[smem] + [vmem] * 14,
+        out_specs=(hbm, vmem, vmem),
         scratch_shapes=[
             pltpu.SMEM((batches + 1,), jnp.int32),
             pltpu.VMEM((points, modes), F32),
             pltpu.VMEM((2 * EDGE * per_point, modes), BF16),
-            pltpu.VMEM((width * BATCH, modes), BF16),
             pltpu.VMEM((width * BATCH, hidden_size), BF16),
-            pltpu.VMEM((slots * BATCH, modes), BF16),
             pltpu.SemaphoreType.DMA(()),
             pltpu.SemaphoreType.DMA((2,)),
-            pltpu.SemaphoreType.DMA(()),
         ],
         compiler_params=pltpu.CompilerParams(vmem_limit_bytes=28 * MIB),
         cost_estimate=pl.CostEstimate(
@@ -338,6 +349,16 @@
         elastic,
         sums,
     )
+    states_next = pl.pallas_call(
+        write_kernel,
+        out_shape=jax.ShapeDtypeStruct((1, rows, modes), BF16),
+        in_specs=[smem, vmem, hbm],
+        out_specs=hbm,
+        scratch_shapes=[pltpu.SMEM((batches + 1,), jnp.int32), pltpu.SemaphoreType.DMA(())],
+        input_output_aliases={2: 0},
+        compiler_params=pltpu.CompilerParams(vmem_limit_bytes=4 * MIB),
+        cost_estimate=pl.CostEstimate(flops=0, bytes_accessed=2 * MIB, transcendentals=0),
+    )(batch_route, updated, states)
     if n // 2 > NEAR_CHIPS:
         everyone = lax.all_gather(residual, "sub", axis=1, tiled=True)[0]
         return states_next, dot(coarse_inverse[0], everyone)[None]

time: 22.7 us -> 21.9 us (0.965)
  waiting for transfers between devices: 4.64 us -> 4.01 us
  starting transfers between devices: 10.6 us -> 10.2 us
    ppermute x3, waiting for transfers between devices: 3.54 us -> 2.9 us  [on_device(): lax.ppermute(pair, 'sub', [(i, i ^ 2 * k) for i in range(n)])]
    pallas_call x0 -> x1, Pallas kernels: none -> 0.62 us  [on_device(): pl.pallas_call(write_kernel, out_shape=jax.ShapeDtypeStruct((1, rows, mod...]
    ppermute x3, starting transfers between devices: 5.13 us -> 4.77 us  [on_device(): lax.ppermute(pair, 'sub', [(i, i ^ 2 * k) for i in range(n)])]
    pallas_call x1, Pallas kernels: 2.62 us -> 2.38 us  [on_device(): pl.pallas_call(functools.partial(plastic_kernel, per_point, width), out_s...]
  transfers between devices with their start and end apart: 6 -> 6, of which waited for: 4 -> 3; matrix products, arithmetic and copies ran while one was open for 0% -> 0% of each run, Pallas kernels for 14% -> 16%
where the time goes in v3:
time: 21.9 us; the launch traced here: 21.8 us
  starting transfers between devices  10.2 us (47%)
  Pallas kernels  6.59 us (30%)
  waiting for transfers between devices  4.01 us (18%)
  between operations  0.85 us (4%)
    ppermute x3, starting transfers between devices, on_device(): lax.ppermute(pair, 'sub', [(i, i ^ 2 * k) for i in range(n)])  4.77 us
    ppermute x1, starting transfers between devices, on_device(): from_core = lax.ppermute(field, 'sub', swap_pairs(n, 0))  4.58 us
    ppermute x3, waiting for transfers between devices, on_device(): lax.ppermute(pair, 'sub', [(i, i ^ 2 * k) for i in range(n)])  2.9 us
    pallas_call x1, Pallas kernels, on_device(): pl.pallas_call(functools.partial(elastic_kernel, per_point), out_shape=(j...  2.86 us
    pallas_call x1, Pallas kernels, on_device(): pl.pallas_call(functools.partial(plastic_kernel, per_point, width), out_s...  2.38 us
    ppermute x1, waiting for transfers between devices, on_device(): other = lax.ppermute(residual, 'sub', swap_pairs(n, 0))  1.1 us
    ppermute x1, starting transfers between devices, on_device(): from_chip = lax.ppermute(field, 'sub', swap_pairs(n, 1))  0.79 us
    pallas_call x1, Pallas kernels, on_device(): pl.pallas_call(coarse_kernel, out_shape=jax.ShapeDtypeStruct((1, points),...  0.71 us
  transfers between devices with their start and end apart: 6, of which 3 were waited for; matrix products, arithmetic and copies ran while one was open for 0% of the time, Pallas kernels for 16%

profile of v3, /device:TPU:0, one launch (start us, length us, event | category | flops | bytes accessed | tf_op | source)
XLA Modules:
  0.0 21.8 jit_solution(8441377910132020979)
XLA Ops:
  0.6 0.0 copy-start
  0.6 0.0 copy-start.3
  0.7 0.0 copy-start.5
  0.7 0.0 copy-start.8
  0.7 0.0 copy-start.10
  0.7 0.8 %collective-permute-start.1 = (f32[6,1,128]{2,1,0:T(1,128)}, f32[6,1,128]{2,1,0:T(1,128)S(1)}, u32[]{:S(2)}, u32[]{:S(2)}) collective-permute-start(f32[6,1,128]{2,1,0:T(1,128)} %bitcast.4), channel_id=1, source_target_pairs={{1,2},{3,4},{5,6},{2,1},{4,3},{6,5},{9,10},{11,12},{13,14},{10,9},... | collective-permute-start | bytes 9224 | tf_op jit(solution)/shard_map/ppermute | solution.py:299
  1.5 4.6 %collective-permute-start = (f32[6,1,128]{2,1,0:T(1,128)}, f32[6,1,128]{2,1,0:T(1,128)S(1)}, u32[]{:S(2)}, u32[]{:S(2)}) collective-permute-start(f32[6,1,128]{2,1,0:T(1,128)} %bitcast.5), channel_id=1, source_target_pairs={{0,1},{2,3},{4,5},{6,7},{1,0},{3,2},{5,4},{7,6},{8,9},{10,11},{12,... | collective-permute-start | bytes 9224 | tf_op jit(solution)/shard_map/ppermute | solution.py:298
  6.1 0.0 copy-start.1
  6.1 0.0 copy-start.2
  6.1 0.0 copy-start.6
  6.1 0.0 copy-start.7
  6.1 0.0 copy-start.9
  6.1 0.0 copy-start.11
  6.2 0.0 copy-done
  6.2 0.0 copy-done.3
  6.2 0.0 copy-done.5
  6.2 0.0 copy-done.8
  6.2 0.0 copy-done.10
  6.2 2.9 %shard_map.132 = (bf16[3072,512]{1,0:T(8,128)(2,1)S(1)}, f32[128,512]{1,0:T(8,128)S(1)}) custom-call(bf16[32,768]{1,0:T(8,128)(2,1)S(1)} %shard_map.131.pick_ref, f32[6,1,128]{2,1,0:T(1,128)S(1)} %bitcast.6, s32[2,128]{1,0:T(2,128)S(1)} %copy-done.10, f32[6,1,512]{2,1,0:T(1,128)S(1)} %bitcast.2, bf16[1,512,512]{2,1,0:T(8,128)(2,1)S(1)} %copy-done.3, ...), custom_call_target="tpu_custom_call" | custom-call | flops 1610612736 | bytes 8388608 | tf_op jit(solution)/shard_map/pallas_call | solution.py:300
  9.1 0.0 collective-permute-done.1.chip_ref
  9.1 0.0 collective-permute-done.core_ref
  9.1 0.0 copy-done.1
  9.1 0.0 copy-done.2
  9.1 0.0 copy-done.6
  9.1 0.0 copy-done.7
  9.1 0.0 copy-done.9
  9.1 0.0 copy-done.11
  9.1 2.4 %shard_map.133 = (bf16[1,3072,512]{2,1,0:T(8,128)(2,1)}, bf16[1,128]{1,0:T(2,128)(2,1)S(1)}, bf16[512,512]{1,0:T(8,128)(2,1)S(1)}) custom-call(s32[1,2,24]{2,1,0:T(2,128)S(1)} %copy-done.7, f32[6,1,128]{2,1,0:T(1,128)S(1)} %collective-permute-done.core_ref, f32[6,1,128]{2,1,0:T(1,128)S(1)} %collective-permute-done.1.chip_ref, f32[6,1,128]{2,1,0:T(1,128)S(1)} %bitcast.7, ...), custom_call_target="tpu_custom_call" | custom-call | flops 2147483648 | bytes 8388608 | tf_op jit(solution)/shard_map/pallas_call | solution.py:314
  11.5 0.1 collective-permute-start.2
  11.6 1.1 %collective-permute-done.2 = bf16[1,128]{1,0:T(2,128)(2,1)S(1)} collective-permute-done((bf16[1,128]{1,0:T(2,128)(2,1)S(1)}, bf16[1,128]{1,0:T(2,128)(2,1)S(1)}, u32[]{:S(2)}, u32[]{:S(2)}) %collective-permute-start.2) | collective-permute-done | bytes 288 | tf_op jit(solution)/shard_map/ppermute | solution.py:365
  12.7 3.8 %collective-permute-start.5 = (bf16[2,128]{1,0:T(2,128)(2,1)S(1)}, bf16[2,128]{1,0:T(2,128)(2,1)S(1)}, u32[]{:S(2)}, u32[]{:S(2)}) collective-permute-start(bf16[2,128]{1,0:T(2,128)(2,1)S(1)} %pad_maximum_fusion.refs_0_), channel_id=1, source_target_pairs={{0,6},{1,7},{2,4},{3,5},{4,2},{5,3},{6,0},{7,1},{8,14},{9,15},{10,... | collective-permute-start | bytes 1544 | tf_op jit(solution)/shard_map/ppermute | solution.py:368
  16.5 1.0 %collective-permute-start.4 = (bf16[2,128]{1,0:T(2,128)(2,1)S(1)}, bf16[2,128]{1,0:T(2,128)(2,1)S(1)}, u32[]{:S(2)}, u32[]{:S(2)}) collective-permute-start(bf16[2,128]{1,0:T(2,128)(2,1)S(1)} %pad_maximum_fusion.refs_0_), channel_id=1, source_target_pairs={{0,4},{1,5},{2,6},{3,7},{4,0},{5,1},{6,2},{7,3},{8,12},{9,13},{10,... | collective-permute-start | bytes 1544 | tf_op jit(solution)/shard_map/ppermute | solution.py:368
  17.5 0.0 collective-permute-start.3
  17.5 0.0 copy-start.4
  17.5 0.6 %shard_map.134 = bf16[1,3072,512]{2,1,0:T(8,128)(2,1)} custom-call(s32[1,2,24]{2,1,0:T(2,128)S(1)} %copy-done.7, bf16[512,512]{1,0:T(8,128)(2,1)S(1)} %get-tuple-element.9.next_ref, bf16[1,3072,512]{2,1,0:T(8,128)(2,1)} %get-tuple-element.10.states_ref), custom_call_target="tpu_custom_call", output_to_operand_aliasing={{}: (2, {})} | custom-call | bytes 2097152 | tf_op jit(solution)/shard_map/pallas_call | solution.py:352
  18.1 0.0 collective-permute-done.5.refs_3_
  18.1 2.8 %collective-permute-done.4.refs_2_ = bf16[2,128]{1,0:T(2,128)(2,1)S(1)} collective-permute-done((bf16[2,128]{1,0:T(2,128)(2,1)S(1)}, bf16[2,128]{1,0:T(2,128)(2,1)S(1)}, u32[]{:S(2)}, u32[]{:S(2)}) %collective-permute-start.4) | collective-permute-done | bytes 544 | tf_op jit(solution)/shard_map/ppermute | solution.py:368
  21.0 0.1 collective-permute-done.3.refs_1_
  21.0 0.0 copy-done.4
  21.0 0.7 %shard_map.135 = f32[1,128]{1,0:T(1,128)} custom-call(bf16[1,128,1024]{2,1,0:T(8,128)(2,1)S(1)} %copy-done.4, bf16[2,128]{1,0:T(2,128)(2,1)S(1)} %pad_maximum_fusion.refs_0_, bf16[2,128]{1,0:T(2,128)(2,1)S(1)} %collective-permute-done.3.refs_1_, bf16[2,128]{1,0:T(2,128)(2,1)S(1)} %collective-permute-done.4.refs_2_, ...), custom_call_target="tpu_custom_call" | custom-call | tf_op jit(solution)/shard_map/pallas_call | solution.py:370
  (2 shorter events, 0.0 us)
Async XLA Ops:
  0.6 5.5 %copy-start = (bf16[1,3072,512]{2,1,0:T(8,128)(2,1)S(1)}, bf16[1,3072,512]{2,1,0:T(8,128)(2,1)}, u32[]{:S(2)}) copy-start(bf16[1,3072,512]{2,1,0:T(8,128)(2,1)} %state_ref.3) | copy-start | bytes 9437188
  0.6 5.5 %copy-start.3 = (bf16[1,512,512]{2,1,0:T(8,128)(2,1)S(1)}, bf16[1,512,512]{2,1,0:T(8,128)(2,1)}, u32[]{:S(2)}) copy-start(bf16[1,512,512]{2,1,0:T(8,128)(2,1)} %stiffness_ref.3) | copy-start | bytes 1572868
  0.7 5.5 %copy-start.5 = (f32[1,6,512]{2,0,1:T(1,128)S(1)}, f32[1,6,512]{2,0,1:T(1,128)}, u32[]{:S(2)}) copy-start(f32[1,6,512]{2,0,1:T(1,128)} %param.15) | copy-start | bytes 36868
  0.7 5.5 %copy-start.8 = (f32[1,6,128]{2,0,1:T(1,128)S(1)}, f32[1,6,128]{2,0,1:T(1,128)}, u32[]{:S(2)}) copy-start(f32[1,6,128]{2,0,1:T(1,128)} %param.12) | copy-start | bytes 9220
  0.7 5.5 %copy-start.10 = (s32[2,128]{1,0:T(2,128)S(1)}, s32[2,128]{1,0:T(2,128)}, u32[]{:S(2)}) copy-start(s32[2,128]{1,0:T(2,128)} %neighbours_ref.3) | copy-start | bytes 3076
  0.7 8.4 %collective-permute-start.1 = (f32[6,1,128]{2,1,0:T(1,128)}, f32[6,1,128]{2,1,0:T(1,128)S(1)}, u32[]{:S(2)}, u32[]{:S(2)}) collective-permute-start(f32[6,1,128]{2,1,0:T(1,128)} %bitcast.4), channel_id=1, source_target_pairs={{1,2},{3,4},{5,6},{2,1},{4,3},{6,5},{9,10},{11,12},{13,14},{10,9},... | collective-permute-start | bytes 9224 | tf_op jit(solution)/shard_map/ppermute | solution.py:299
  1.5 7.6 %collective-permute-start = (f32[6,1,128]{2,1,0:T(1,128)}, f32[6,1,128]{2,1,0:T(1,128)S(1)}, u32[]{:S(2)}, u32[]{:S(2)}) collective-permute-start(f32[6,1,128]{2,1,0:T(1,128)} %bitcast.5), channel_id=1, source_target_pairs={{0,1},{2,3},{4,5},{6,7},{1,0},{3,2},{5,4},{7,6},{8,9},{10,11},{12,... | collective-permute-start | bytes 9224 | tf_op jit(solution)/shard_map/ppermute | solution.py:298
  6.1 3.0 %copy-start.1 = (bf16[1,512,2048]{2,1,0:T(8,128)(2,1)S(1)}, bf16[1,512,2048]{2,1,0:T(8,128)(2,1)}, u32[]{:S(2)}) copy-start(bf16[1,512,2048]{2,1,0:T(8,128)(2,1)} %expand_ref.1) | copy-start | bytes 6291460
  6.1 3.0 %copy-start.2 = (bf16[1,2048,512]{2,1,0:T(8,128)(2,1)S(1)}, bf16[1,2048,512]{2,1,0:T(8,128)(2,1)}, u32[]{:S(2)}) copy-start(bf16[1,2048,512]{2,1,0:T(8,128)(2,1)} %contract_ref.1) | copy-start | bytes 6291460
  6.1 3.0 %copy-start.6 = (s32[1,3072]{1,0:T(1,128)S(1)}, s32[1,3072]{1,0:T(1,128)}, u32[]{:S(2)}) copy-start(s32[1,3072]{1,0:T(1,128)} %flags_ref.1) | copy-start | bytes 36868
  6.1 3.0 %copy-start.7 = (s32[1,2,24]{2,1,0:T(2,128)S(1)}, s32[1,2,24]{2,1,0:T(2,128)}, u32[]{:S(2)}) copy-start(s32[1,2,24]{2,1,0:T(2,128)} %route_ref.3) | copy-start | bytes 580
  6.1 3.0 %copy-start.9 = (bf16[1,512]{1,0:T(2,128)(2,1)S(1)}, bf16[1,512]{1,0:T(2,128)(2,1)}, u32[]{:S(2)}) copy-start(bf16[1,512]{1,0:T(2,128)(2,1)} %readout_ref.1) | copy-start | bytes 3076
  6.1 3.0 %copy-start.11 = (f32[1,128]{1,0:T(1,128)S(1)}, f32[1,128]{1,0:T(1,128)}, u32[]{:S(2)}) copy-start(f32[1,128]{1,0:T(1,128)} %force_ref.1) | copy-start | bytes 1540
  11.5 1.2 %collective-permute-start.2 = (bf16[1,128]{1,0:T(2,128)(2,1)S(1)}, bf16[1,128]{1,0:T(2,128)(2,1)S(1)}, u32[]{:S(2)}, u32[]{:S(2)}) collective-permute-start(bf16[1,128]{1,0:T(2,128)(2,1)S(1)} %get-tuple-element.11), channel_id=1, source_target_pairs={{0,1},{2,3},{4,5},{6,7},{1,0},{3,2},{5,4},{7,6},{8,9},{10,11},{12,... | collective-permute-start | bytes 776 | tf_op jit(solution)/shard_map/ppermute | solution.py:365
  12.7 5.4 %collective-permute-start.5 = (bf16[2,128]{1,0:T(2,128)(2,1)S(1)}, bf16[2,128]{1,0:T(2,128)(2,1)S(1)}, u32[]{:S(2)}, u32[]{:S(2)}) collective-permute-start(bf16[2,128]{1,0:T(2,128)(2,1)S(1)} %pad_maximum_fusion.refs_0_), channel_id=1, source_target_pairs={{0,6},{1,7},{2,4},{3,5},{4,2},{5,3},{6,0},{7,1},{8,14},{9,15},{10,... | collective-permute-start | bytes 1544 | tf_op jit(solution)/shard_map/ppermute | solution.py:368
  16.5 4.4 %collective-permute-start.4 = (bf16[2,128]{1,0:T(2,128)(2,1)S(1)}, bf16[2,128]{1,0:T(2,128)(2,1)S(1)}, u32[]{:S(2)}, u32[]{:S(2)}) collective-permute-start(bf16[2,128]{1,0:T(2,128)(2,1)S(1)} %pad_maximum_fusion.refs_0_), channel_id=1, source_target_pairs={{0,4},{1,5},{2,6},{3,7},{4,0},{5,1},{6,2},{7,3},{8,12},{9,13},{10,... | collective-permute-start | bytes 1544 | tf_op jit(solution)/shard_map/ppermute | solution.py:368
  17.5 3.5 %collective-permute-start.3 = (bf16[2,128]{1,0:T(2,128)(2,1)S(1)}, bf16[2,128]{1,0:T(2,128)(2,1)S(1)}, u32[]{:S(2)}, u32[]{:S(2)}) collective-permute-start(bf16[2,128]{1,0:T(2,128)(2,1)S(1)} %pad_maximum_fusion.refs_0_), channel_id=1, source_target_pairs={{0,2},{1,3},{2,0},{3,1},{4,6},{5,7},{6,4},{7,5},{8,10},{9,11},{10,... | collective-permute-start | bytes 1544 | tf_op jit(solution)/shard_map/ppermute | solution.py:368
  17.5 3.5 %copy-start.4 = (bf16[1,128,1024]{2,1,0:T(8,128)(2,1)S(1)}, bf16[1,128,1024]{2,1,0:T(8,128)(2,1)}, u32[]{:S(2)}) copy-start(bf16[1,128,1024]{2,1,0:T(8,128)(2,1)} %inverse_ref.1) | copy-start | bytes 786436
